TPU v7x, 32 devices: a whole 2x2x4 slice. The times are simulated.
32 devices in a mesh: dp: 8 (over z, y), seq: 4 (over x, core).
Axes of the slice: x: 2, y: 2, z: 4, core: 2. Of those that a mesh axis runs over, the one named last changes fastest.
Arguments:
- hidden_in: bfloat16 [1024, 24, 256], P('seq', 'dp'), may hold values from -6 to 6
- embedding: bfloat16 [1024, 24, 256], P('seq', 'dp'), may hold values from -6 to 6
- lengths: int32 [24], P('dp'), may hold values from 128 to 1024, as said below
- cotangent: bfloat16 [1024, 24, 256], P('seq', 'dp'), may hold values from -6 to 6
- ln1_gain: float32 [256], replicated, may hold values from 0.1 to 1.9
- ln1_bias: float32 [256], replicated, may hold values from -1.75 to 1.75
- qkv_weight: bfloat16 [256, 768], replicated, may hold values from -0.5 to 0.5
- qv_bias: float32 [2, 256], replicated, may hold values from -1.75 to 1.75
- out_weight: bfloat16 [256, 256], replicated, may hold values from -4 to 4
- out_bias: float32 [256], replicated, may hold values from -1.75 to 1.75
- ln2_gain: float32 [256], replicated, may hold values from 0.1 to 1.9
- ln2_bias: float32 [256], replicated, may hold values from -1.75 to 1.75
- up_weight: bfloat16 [256, 1024], replicated, may hold values from -0.375 to 0.375
- up_bias: float32 [1024], replicated, may hold values from -1.75 to 1.75
- down_weight: bfloat16 [1024, 256], replicated, may hold values from -0.1875 to 0.1875
- down_bias: float32 [256], replicated, may hold values from -1.75 to 1.75
Outputs:
- output: bfloat16 [1024, 24, 256], P('seq', 'dp')
- grad_hidden: float32 [1024, 24, 256], P('seq', 'dp')
- grad_embed: float32 [1024, 24, 256], P('seq', 'dp')
- grad_ln1_gain: float32 [256], replicated
- grad_ln1_bias: float32 [256], replicated
- grad_qkv_weight: float32 [256, 768], replicated
- grad_qv_bias: float32 [2, 256], replicated
- grad_out_weight: float32 [256, 256], replicated
- grad_out_bias: float32 [256], replicated
- grad_ln2_gain: float32 [256], replicated
- grad_ln2_bias: float32 [256], replicated
- grad_up_weight: float32 [256, 1024], replicated
- grad_up_bias: float32 [1024], replicated
- grad_down_weight: float32 [1024, 256], replicated
- grad_down_bias: float32 [256], replicated
Inputs may be any that keep to these rules, and one draw needn't show every extreme that they name: `lengths`: among each dp index's 3 rows (aligned blocks of 3), one row, drawn from the seed, has length 1024; positions at or past a row's length are padding keys.
All inputs are finite; a program needn't handle non-finite values.
Results may differ from a plain program's by a relative error of at most 0.022.
The roundings to bfloat16 on the way count: a program that leaves them out, or rounds other values in their place, can miss the bound.
Values may be sent and summed in bfloat16 or wider, within the bound.
A program may use at most 128 MiB of HBM per device.

v0:
```python
import functools

import jax
import jax.numpy as jnp
from jax import lax
from jax.experimental import pallas as pl
from jax.experimental.pallas import tpu as pltpu
from jax.sharding import PartitionSpec as P

EPS = 1e-05
MASKED = -1e30
HEADS = 4
BF = jnp.bfloat16
F32 = jnp.float32
MESH = pl.DeviceIdType.MESH


def nn(a, b):
    return lax.dot_general(a, b, (((1,), (0,)), ((), ())), preferred_element_type=F32)


def nt(a, b):
    return lax.dot_general(a, b, (((1,), (1,)), ((), ())), preferred_element_type=F32)


def normalise(x):
    mean = jnp.mean(x, axis=-1, keepdims=True)
    centred = x - mean
    rstd = lax.rsqrt(jnp.mean(centred * centred, axis=-1, keepdims=True) + EPS)
    return centred * rstd, rstd


def norm_back(grad, gain, xhat, rstd):
    gl = grad * gain
    m1 = jnp.mean(gl, axis=-1, keepdims=True)
    m2 = jnp.mean(gl * xhat, axis=-1, keepdims=True)
    return rstd * (gl - m1 - xhat * m2)


def fold(x):
    return jnp.sum(x.reshape(x.shape[0] // 8, 8, x.shape[1]), axis=0)


def gelu_parts(x):
    c0 = 0.7978845608028654
    x2 = x * x
    t = jnp.tanh(c0 * (x + 0.044715 * (x2 * x)))
    half = 0.5 * (1.0 + t)
    slope = half + (0.5 * x) * (1.0 - t * t) * (c0 * (1.0 + (3 * 0.044715) * x2))
    return x * half, slope


HD = 64


def head_rows(x, h):
    own = x[h * HD:(h + 1) * HD]
    zero = jnp.zeros_like(own)
    return jnp.concatenate([own, zero] if h % 2 == 0 else [zero, own], axis=0)


def pair(h):
    return slice((h // 2) * 2 * HD, (h // 2 + 1) * 2 * HD)


def block_kernel(cfg, *refs):
    S, DP, R, L, D, FF, reduce_here = cfg
    W = 3 * D + D + 2 * FF
    UP, DN, OW, QW = 0, FF, 2 * FF, 2 * FF + D
    (hid_ref, emb_ref, cot_ref, len_ref, ln1g_ref, ln1b_ref, wqkv_ref, qvb_ref, wout_ref, bout_ref, ln2g_ref, ln2b_ref,
     wup_ref, bup_ref, wdn_ref, bdn_ref,
     y_ref, g1_ref, ge_ref, gw_ref, gv_ref,
     wT, bcol, stream, gstream, gmid, nall, xh1, rs1, xh2, rs2, n2T, qT_s, qn_s, linv, oT_s, hid_s, slope_s,
     e_scr, pg_out, pg_in, vec, *comm) = refs
    nsend, nrecv, psend, precv, out_sem = comm[:5]
    me = lax.axis_index("seq")
    dp = lax.axis_index("dp")
    mine = pl.ds(pl.multiple_of(me * L, L), L)

    def at(s):
        return (dp, s)

    barrier = pltpu.get_barrier_semaphore()
    for k in range(1, S):
        pl.semaphore_signal(barrier, inc=1, device_id=(dp, lax.rem(me + k, S)), device_id_type=MESH)
    peers = S - 1
    if reduce_here:
        for k in range(1, DP):
            pl.semaphore_signal(barrier, inc=1, device_id=(lax.rem(dp + k, DP), me), device_id_type=MESH)
        peers += DP - 1
    pl.semaphore_wait(barrier, peers)

    ln1g, ln1b = ln1g_ref[...], ln1b_ref[...]
    ln2g, ln2b = ln2g_ref[...], ln2b_ref[...]

    def normed_copy(a, r, src, dst):
        rows = pl.ds(pl.multiple_of(src * L, L), L)
        return pltpu.make_async_remote_copy(
            src_ref=nall.at[a, r, rows], dst_ref=nall.at[a, r, rows], send_sem=nsend.at[a, r, dst],
            recv_sem=nrecv.at[a, r, src], device_id=at(dst), device_id_type=MESH)

    def part_copy(a, r, src, dst):
        return pltpu.make_async_remote_copy(
            src_ref=pg_out.at[a, r, dst], dst_ref=pg_in.at[a, r, src - 1], send_sem=psend.at[a, r, dst],
            recv_sem=precv.at[a, r, src], device_id=at(dst), device_id_type=MESH)

    def first_norm(a, r):
        u = stream[r] + emb_ref[r].astype(F32)
        stream[r] = u
        xhat, rstd = normalise(u)
        xh1[a, r] = xhat
        rs1[a, r] = jnp.broadcast_to(rstd, (L, 128))
        nall[a, r, mine] = (xhat * ln1g + ln1b).astype(BF)

        @pl.loop(me + 1, S)
        def _(dst):
            normed_copy(a, r, me, dst).start()

    @pl.loop(0, R)
    def _(r):
        stream[r] = hid_ref[r].astype(F32)
        first_norm(0, r)

    for k in range(3):
        wT[k] = wqkv_ref[:, k * D:(k + 1) * D].T
    for k in range(2):
        bcol[k] = jnp.broadcast_to(qvb_ref[k:k + 1, :], (128, D)).T
    bq = jnp.concatenate([bcol[0]] * (L // 128), axis=1)
    bv = jnp.concatenate([bcol[1]] * (L // 128), axis=1)

    vec[...] = jnp.zeros_like(vec)

    def forward(a, r, VT, s_scr, m_scr, l_scr, oacc):
        normed = nall[a, r, mine]
        qT = ((nt(wT[0], normed) + bq) * (HD ** -0.5)).astype(BF)
        qn_s[a, r] = qT.T
        qT_s[...] = qT
        m_scr[...] = jnp.full_like(m_scr, MASKED)
        l_scr[...] = jnp.zeros_like(l_scr)
        oacc[...] = jnp.zeros_like(oacc)
        length = len_ref[r]

        @pl.loop(0, me + 1)
        def _(t):
            @pl.when(t < me)
            def _():
                normed_copy(a, r, t, me).wait_recv()

            rows = nall[a, r, pl.ds(pl.multiple_of(t * L, L), L)]
            keys = nn(rows, wqkv_ref[:, D:2 * D]).astype(BF)
            VT[t] = (nt(wT[2], rows) + bv).astype(BF)
            key_pos = t * L + lax.broadcasted_iota(jnp.int32, (L, L), 0)
            query_pos = me * L + lax.broadcasted_iota(jnp.int32, (L, L), 1)
            bias = jnp.where((key_pos <= query_pos) & (key_pos < length), 0.0, MASKED)
            for h in range(HEADS):
                s = nn(keys[:, pair(h)], head_rows(qT_s[...], h)) + bias
                s_scr[t, h] = s
                m_scr[h] = jnp.maximum(m_scr[h], jnp.max(s.reshape(L // 8, 8, L), axis=0))

        for h in range(HEADS):
            m_scr[h] = jnp.broadcast_to(jnp.max(m_scr[h], axis=0, keepdims=True), (8, L))

        @pl.loop(0, me + 1)
        def _(t):
            for h in range(HEADS):
                e = jnp.exp(s_scr[t, h] - m_scr[h, 0:1])
                l_scr[h] += fold(e)
                low = e.astype(BF)
                e_scr[a, r, t, h] = low
                oacc[h * HD:(h + 1) * HD] += nn(VT[t, h * HD:(h + 1) * HD, :], low)

        heads = []
        for h in range(HEADS):
            inv = 1.0 / jnp.sum(l_scr[h], axis=0, keepdims=True)
            linv[a, r, h] = jnp.broadcast_to(inv, (8, L))
            heads.append(oacc[h * HD:(h + 1) * HD] * inv)
        oT = jnp.concatenate(heads, axis=0).astype(BF)
        oT_s[a, r] = oT
        middle = stream[r] + (nn(oT.T, wout_ref[...]) + bout_ref[...])
        xhat, rstd = normalise(middle)
        xh2[a, r] = xhat
        rs2[a, r] = jnp.broadcast_to(rstd, (L, 128))
        normed2 = (xhat * ln2g + ln2b).astype(BF)
        n2T[a, r] = normed2.T
        hidden, slope = gelu_parts(nn(normed2, wup_ref[...]) + bup_ref[...])
        hidden = hidden.astype(BF)
        hid_s[a, r] = hidden
        slope_s[a, r] = slope
        stream[r] = middle + (nn(hidden, wdn_ref[...]) + bdn_ref[...])

    def forward_all(*scr):
        @pl.loop(0, 2 * R)
        def _(n):
            a, r = lax.div(n, R), lax.rem(n, R)
            forward(a, r, *scr)

            @pl.when(a == 0)
            def _():
                first_norm(1, r)

            @pl.when(a == 1)
            def _():
                y_ref[r] = stream[r].astype(BF)
                gstream[r] = cot_ref[r].astype(F32)

    VM = pltpu.VMEM
    pl.run_scoped(forward_all, VM((S, D, L), BF), VM((S, HEADS, L, L), F32), VM((HEADS, 8, L), F32), VM((HEADS, 8, L), F32),
                  VM((D, L), F32))
    pl.run_scoped(functools.partial(backward_kernel, cfg, refs, me, dp, mine, normed_copy, part_copy),
                  VM((D, L), F32), VM((R, D, L), BF), VM((R, L, FF), BF), VM((R, L, D), BF), VM((R, L, 3 * D), BF),
                  VM((D, W), F32))


def backward_kernel(cfg, refs, me, dp, mine, normed_copy, part_copy, gqacc, gbT, gpre, ga_s, gqkv, dW):
    S, DP, R, L, D, FF, reduce_here = cfg
    W = 3 * D + D + 2 * FF
    UP, DN, OW, QW = 0, FF, 2 * FF, 2 * FF + D
    (hid_ref, emb_ref, cot_ref, len_ref, ln1g_ref, ln1b_ref, wqkv_ref, qvb_ref, wout_ref, bout_ref, ln2g_ref, ln2b_ref,
     wup_ref, bup_ref, wdn_ref, bdn_ref,
     y_ref, g1_ref, ge_ref, gw_ref, gv_ref,
     wT, bcol, stream, gstream, gmid, nall, xh1, rs1, xh2, rs2, n2T, qT_s, qn_s, linv, oT_s, hid_s, slope_s,
     e_scr, pg_out, pg_in, vec, *comm) = refs
    nsend, nrecv, psend, precv, out_sem = comm[:5]
    ln1g, ln2g = ln1g_ref[...], ln2g_ref[...]

    def add_vec(start, terms):
        vec[:, start:start + terms.shape[1]] += fold(terms)

    V_LN1G, V_LN1B, V_QB, V_VB, V_OB, V_LN2G, V_LN2B, V_DB, V_UB = [D * k for k in range(9)]

    lane = lax.broadcasted_iota(jnp.int32, (L, 2 * HD), 1)

    def head_lanes(x, h):
        keep = (lane < HD) if h % 2 == 0 else (lane >= HD)
        return jnp.where(keep, x[:, pair(h)], jnp.zeros((), x.dtype))

    def backward_mlp(a, r):
        g = gstream[r]
        gb = g.astype(BF)
        add_vec(V_DB, gb.astype(F32))
        gbT[r] = gb.T
        pre = (nt(gb, wdn_ref[...]) * slope_s[a, r]).astype(BF)
        gpre[r] = pre
        add_vec(V_UB, pre.astype(F32))
        gn2 = nt(pre, wup_ref[...])
        xhat = xh2[a, r]
        add_vec(V_LN2G, gn2 * xhat)
        add_vec(V_LN2B, gn2)
        rstd = jnp.concatenate([rs2[a, r]] * (D // 128), axis=1)
        gm = g + norm_back(gn2, ln2g, xhat, rstd)
        gmid[r] = gm
        ga = gm.astype(BF)
        ga_s[r] = ga
        add_vec(V_OB, ga.astype(F32))

    def backward_attention(a, r):
        gaT = nt(wout_ref[...], ga_s[r]).astype(BF).astype(F32)
        oT = oT_s[a, r].astype(F32)
        scaled, deltas = [], []
        for h in range(HEADS):
            hs = slice(h * HD, (h + 1) * HD)
            inv = linv[a, r, h, 0:1]
            part = gaT[hs] * inv
            scaled.append(part.astype(BF))
            deltas.append(jnp.sum(part * oT[hs], axis=0, keepdims=True))
        gaT_n = jnp.concatenate(scaled, axis=0)
        ga_n = gaT_n.T
        queries = qn_s[a, r]
        gqacc[...] = jnp.zeros_like(gqacc)

        @pl.loop(0, me + 1)
        def _(t):
            rows = nall[a, r, pl.ds(pl.multiple_of(t * L, L), L)]
            values = (nn(rows, wqkv_ref[:, 2 * D:]) + qvb_ref[1:2, :]).astype(BF)
            KT = nt(wT[1], rows).astype(BF)
            gk, gv = [], []
            for h in range(HEADS):
                hs = slice(h * HD, (h + 1) * HD)
                gp = nn(values[:, pair(h)], head_rows(gaT_n, h))
                low = e_scr[a, r, t, h]
                ds = (low.astype(F32) * (gp - deltas[h])).astype(BF)
                gk.append(nn(ds, head_lanes(queries, h)))
                gv.append(nn(low, head_lanes(ga_n, h)))
                gqacc[hs] += nn(KT[hs], ds)
            gkv = jnp.concatenate([gk[0] + gk[1], gk[2] + gk[3], gv[0] + gv[1], gv[2] + gv[3]], axis=1).astype(BF)
            add_vec(V_VB, gkv[:, D:].astype(F32))
            dW[:, QW + D:QW + 3 * D] += nn(rows.T, gkv)

            @pl.when(t < me)
            def _():
                pg_out[a, r, t] = nt(gkv, wqkv_ref[:, D:]).astype(BF)
                part_copy(a, r, me, t).start()

            @pl.when(t == me)
            def _():
                gqkv[r, :, D:] = gkv

        gq = (gqacc[...] * (HD ** -0.5)).T.astype(BF)
        gqkv[r, :, :D] = gq
        add_vec(V_QB, gq.astype(F32))

    def backward_norm(a, r):
        gn = nt(gqkv[r], wqkv_ref[...])
        gmid_r = gmid[r]

        def add(s, total):
            part_copy(a, r, s, me).wait_recv()
            return total + pg_in[a, r, s - 1].astype(F32)

        gn = lax.fori_loop(me + 1, S, add, gn)
        xhat = xh1[a, r]
        add_vec(V_LN1G, gn * xhat)
        add_vec(V_LN1B, gn)
        rstd = jnp.concatenate([rs1[a, r]] * (D // 128), axis=1)
        gstream[r] = gmid_r + norm_back(gn, ln1g, xhat, rstd)

    def weight_terms(a, first):
        def put(start, value):
            if first:
                dW[:, start:start + value.shape[1]] = value
            else:
                dW[:, start:start + value.shape[1]] += value

        put(UP, sum(nn(n2T[a, r], gpre[r]) for r in range(R)))
        put(DN, sum(nn(gbT[r], hid_s[a, r]) for r in range(R)))
        put(OW, sum(nn(oT_s[a, r], ga_s[r]) for r in range(R)))

    def query_terms(a, first):
        value = sum(nn(nall[a, r, mine].T, gqkv[r, :, :D]) for r in range(R))
        if first:
            dW[:, QW:QW + D] = value
        else:
            dW[:, QW:QW + D] += value

    dW[:, QW + D:QW + 3 * D] = jnp.zeros((D, 2 * D), F32)
    for a in (1, 0):
        @pl.loop(0, R)
        def _(r):
            backward_mlp(a, r)

        weight_terms(a, a == 1)

        @pl.loop(0, R)
        def _(r):
            backward_attention(a, r)

        query_terms(a, a == 1)

        @pl.loop(0, R)
        def _(r):
            backward_norm(a, r)
            if a == 1:
                g1_ref[r] = gstream[r]
            else:
                g = gstream[r]
                ge_ref[r] = g + g1_ref[r]
                g1_ref[r] = g

    sums = jnp.sum(vec[...], axis=0, keepdims=True)
    if reduce_here:
        stage, seq_in, mid, dp_in, gath, vs, vs_seq, vs_dp, ss, sr, ds_, dr, gs, gr, fs, fr, vss, vsr, vds, vdr = comm[5:]
        rows = D // S
        groups = min(DP, rows // 16)
        lanes = W // (DP // groups)
        crow = rows // groups
        stage[...] = dW[...].astype(BF)

        def rows_of(s):
            return pl.ds(pl.multiple_of(s * rows, rows), rows)

        for k in range(W // 128):
            vs[k:k + 1, :] = sums[:, k * 128:(k + 1) * 128]

        def seq_copy(k):
            dst = lax.rem(me + k, S)
            return pltpu.make_async_remote_copy(
                src_ref=stage.at[rows_of(dst)], dst_ref=seq_in.at[k - 1], send_sem=ss.at[k - 1], recv_sem=sr.at[k - 1],
                device_id=(dp, dst), device_id_type=MESH)

        def vseq_copy(k):
            dst = lax.rem(me + k, S)
            return pltpu.make_async_remote_copy(
                src_ref=vs, dst_ref=vs_seq.at[me], send_sem=vss.at[k - 1], recv_sem=vsr.at[k - 1],
                device_id=(dp, dst), device_id_type=MESH)

        for k in range(1, S):
            vseq_copy(k).start()
            seq_copy(k).start()
        vs_seq[me] = vs[...]
        for k in range(1, S):
            vseq_copy(k).wait()
        total = vs_seq[0]
        for s in range(1, S):
            total = total + vs_seq[s]
        vs_dp[dp] = total

        def vdp_copy(k):
            dst = lax.rem(dp + k, DP)
            return pltpu.make_async_remote_copy(
                src_ref=vs_dp.at[dp], dst_ref=vs_dp.at[dp], send_sem=vds.at[k - 1], recv_sem=vdr.at[k - 1],
                device_id=(dst, me), device_id_type=MESH)

        for k in range(1, DP):
            vdp_copy(k).start()
        for k in range(1, S):
            seq_copy(k).wait()
        acc = dW[rows_of(me), :]
        for k in range(1, S):
            acc = acc + seq_in[k - 1].astype(F32)
        dW[rows_of(me), :] = acc
        mid[...] = acc.astype(BF)

        def chunk(d):
            rg, lg = lax.div(d, DP // groups), lax.rem(d, DP // groups)
            return pl.ds(pl.multiple_of(rg * crow, crow), crow), pl.ds(pl.multiple_of(lg * lanes, 128), lanes)

        def dp_copy(k):
            dst = lax.rem(dp + k, DP)
            cr, cl = chunk(dst)
            return pltpu.make_async_remote_copy(
                src_ref=mid.at[cr, cl], dst_ref=dp_in.at[k - 1], send_sem=ds_.at[k - 1], recv_sem=dr.at[k - 1],
                device_id=(dst, me), device_id_type=MESH)

        for k in range(1, DP):
            dp_copy(k).start()
        for k in range(1, DP):
            vdp_copy(k).wait()
        total = vs_dp[0]
        for s in range(1, DP):
            total = total + vs_dp[s]
        gv_ref[...] = total
        for k in range(1, DP):
            dp_copy(k).wait()
        rg, lg = lax.div(dp, DP // groups), lax.rem(dp, DP // groups)
        cr = pl.ds(pl.multiple_of(me * rows + rg * crow, crow), crow)
        cl = pl.ds(pl.multiple_of(lg * lanes, 128), lanes)
        acc = dW[cr, cl]
        for k in range(1, DP):
            acc = acc + dp_in[k - 1].astype(F32)
        gath[cr, cl] = acc.astype(BF)

        def back_copy(k):
            dst = lax.rem(dp + k, DP)
            return pltpu.make_async_remote_copy(
                src_ref=gath.at[cr, cl], dst_ref=gath.at[cr, cl], send_sem=gs.at[k - 1], recv_sem=gr.at[k - 1],
                device_id=(dst, me), device_id_type=MESH)

        for k in range(1, DP):
            back_copy(k).start()
        for k in range(1, DP):
            back_copy(k).wait()

        def full_copy(k):
            dst = lax.rem(me + k, S)
            return pltpu.make_async_remote_copy(
                src_ref=gath.at[rows_of(me)], dst_ref=gath.at[rows_of(me)], send_sem=fs.at[k - 1], recv_sem=fr.at[k - 1],
                device_id=(dp, dst), device_id_type=MESH)

        for k in range(1, S):
            full_copy(k).start()
        for k in range(1, S):
            full_copy(k).wait()
        out = pltpu.make_async_copy(gath, gw_ref, out_sem)
        out.start()
        out.wait()
    else:
        out = pltpu.make_async_copy(dW, gw_ref, out_sem)
        out.start()
        out.wait()
        for k in range(W // 128):
            gv_ref[k:k + 1, :] = sums[:, k * 128:(k + 1) * 128]

    for a in range(2):
        for r in range(R):
            @pl.loop(me + 1, S)
            def _(dst):
                normed_copy(a, r, me, dst).wait_send()

            @pl.loop(0, me)
            def _(dst):
                part_copy(a, r, me, dst).wait_send()


def solution(mesh):
    S, DP = mesh.shape["seq"], mesh.shape["dp"]

    def shards(hidden_in, embedding, lengths, cotangent, ln1_gain, ln1_bias, qkv_weight, qv_bias, out_weight, out_bias,
               ln2_gain, ln2_bias, up_weight, up_bias, down_weight, down_bias):
        L, R, D = hidden_in.shape
        FF = up_weight.shape[1]
        W = 4 * D + 2 * FF
        rows = D // S
        groups = min(DP, rows // 16)
        reduce_here = rows % 16 == 0 and DP % groups == 0 and rows % (16 * groups) == 0 and W % (128 * (DP // groups)) == 0
        cfg = (S, DP, R, L, D, FF, reduce_here)
        lanes = W // (DP // groups)
        crow = rows // groups
        VM = pltpu.VMEM
        DMA = pltpu.SemaphoreType.DMA
        scratch = [
            VM((3, D, D), BF), VM((2, D, 128), F32), VM((R, L, D), F32), VM((R, L, D), F32), VM((R, L, D), F32),
            VM((2, R, S * L, D), BF), VM((2, R, L, D), F32), VM((2, R, L, 128), F32), VM((2, R, L, D), F32),
            VM((2, R, L, 128), F32), VM((2, R, D, L), BF), VM((D, L), BF), VM((2, R, L, D), BF),
            VM((2, R, HEADS, 8, L), F32), VM((2, R, D, L), BF), VM((2, R, L, FF), BF), VM((2, R, L, FF), F32),
            VM((2, R, S, HEADS, L, L), BF), VM((2, R, S - 1, L, D), BF), VM((2, R, S - 1, L, D), BF), VM((8, W), F32),
            DMA((2, R, S)), DMA((2, R, S)), DMA((2, R, S)), DMA((2, R, S)), DMA,
        ]
        if reduce_here:
            scratch += [
                VM((D, W), BF), VM((S - 1, rows, W), BF), VM((rows, W), BF), VM((DP - 1, crow, lanes), BF), VM((D, W), BF),
                VM((W // 128, 128), F32), VM((S, W // 128, 128), F32), VM((DP, W // 128, 128), F32),
                DMA((S - 1,)), DMA((S - 1,)), DMA((DP - 1,)), DMA((DP - 1,)), DMA((DP - 1,)), DMA((DP - 1,)),
                DMA((S - 1,)), DMA((S - 1,)), DMA((S - 1,)), DMA((S - 1,)), DMA((DP - 1,)), DMA((DP - 1,)),
            ]
        vm = pl.BlockSpec(memory_space=pltpu.VMEM)
        sm = pl.BlockSpec(memory_space=pltpu.SMEM)
        rows_first = lambda x: jnp.transpose(x, (1, 0, 2))
        line = lambda x: x.reshape(1, -1)
        y, g1, ge, gw, gv = pl.pallas_call(
            functools.partial(block_kernel, cfg),
            out_shape=(
                jax.ShapeDtypeStruct((R, L, D), BF), jax.ShapeDtypeStruct((R, L, D), F32),
                jax.ShapeDtypeStruct((R, L, D), F32), jax.ShapeDtypeStruct((D, W), BF if reduce_here else F32),
                jax.ShapeDtypeStruct((W // 128, 128), F32)),
            in_specs=[vm, vm, vm, sm] + [vm] * 12,
            out_specs=(vm, vm, vm, pl.BlockSpec(memory_space=pl.ANY), vm),
            scratch_shapes=scratch,
            compiler_params=pltpu.CompilerParams(
                collective_id=0, has_side_effects=True, vmem_limit_bytes=VMEM_LIMIT),
        )(rows_first(hidden_in), rows_first(embedding), rows_first(cotangent), lengths, line(ln1_gain), line(ln1_bias),
          qkv_weight, qv_bias, out_weight, line(out_bias), line(ln2_gain), line(ln2_bias), up_weight, line(up_bias),
          down_weight, line(down_bias))
        gv = gv.reshape(-1)
        if not reduce_here:
            gw, gv = lax.psum((gw, gv), ("dp", "seq"))
        gw = gw.astype(F32)
        part = lambda k, n=1: gv[k * D:(k + n) * D]
        return (
            rows_first(y), rows_first(g1), rows_first(ge), part(0), part(1), gw[:, 2 * FF + D:], part(2, 2).reshape(2, D),
            gw[:, 2 * FF:2 * FF + D], part(4), part(5), part(6), gw[:, :FF], part(8, FF // D), gw[:, FF:2 * FF].T, part(7))

    token = P("seq", "dp", None)
    return jax.shard_map(
        shards, mesh=mesh, in_specs=(token, token, P("dp"), token) + (P(),) * 12, out_specs=(token,) * 3 + (P(),) * 12,
        check_vma=False)


VMEM_LIMIT = 62 * 1024 * 1024
```

profile of v0, /device:TPU:0, one launch (start us, length us, event | category | flops | bytes accessed | tf_op | source)
XLA Modules:
  0.0 165.1 jit_solution(9765815090256166862)
XLA Ops:
  0.7 152.4 %shard_map.271 = (bf16[3,256,256]{2,1,0:T(8,128)(2,1)}, f32[3,256,256]{2,1,0:T(8,128)}, f32[3,256,256]{2,1,0:T(8,128)}, bf16[256,3072]{1,0:T(8,128)(2,1)}, f32[24,128]{1,0:T(8,128)}) custom-call(bf16[3,256,256]{2,1,0:T(8,128)(2,1)} %bitcast.31, bf16[3,256,256]{2,1,0:T(8,128)(2,1)} %bitcast.32, bf16[3,256,256]{2,1,0:T(8,128)(2,1)} %bitcast.33, s32[3]{0:T(128)} %refs_3_.1, ...), custom_call_target="tpu_custom_call" | custom-call | tf_op jit(solution)/shard_map/pallas_call | solution.py:519
  153.0 1.4 slice_bitcast_fusion.2
  154.5 1.8 %convert_element_type.3 = f32[256,3072]{1,0:T(8,128)S(1)} convert(bf16[256,3072]{1,0:T(8,128)(2,1)} %get-tuple-element.24) | non-fusion elementwise | flops 786432 | bytes 4718592 | tf_op jit(solution)/shard_map/convert_element_type | solution.py:536
  156.2 0.0 copy-start
  156.2 0.1 slice_bitcast_fusion
  156.3 0.0 copy-start.3
  156.4 0.0 copy-start.2
  156.4 1.3 copy.31
  157.7 0.0 copy-done
  157.7 0.0 copy-start.1
  157.7 1.1 slice.79
  158.8 0.9 slice.77
  159.7 0.7 slice.78
  160.4 0.0 copy-done.3
  160.4 0.6 reshape.71
  161.0 0.6 slice_bitcast_fusion.1
  161.6 1.8 %copy.35 = bf16[256,3,256]{2,0,1:T(8,128)(2,1)} copy(bf16[256,3,256]{2,0,1:T(8,128)(2,1)} %bitcast.34) | data formatting | bytes 786432
  163.4 0.0 copy-done.2
  163.4 0.9 copy.36
  164.3 0.0 copy-done.1
  164.3 0.9 copy.37
  (1 shorter events, 0.0 us)
Async XLA Ops:
  156.2 1.5 copy-start
  156.3 4.1 %copy-start.3 = (f32[24,128]{1,0:T(8,128)S(1)}, f32[24,128]{1,0:T(8,128)}, u32[]{:S(2)}) copy-start(f32[24,128]{1,0:T(8,128)} %get-tuple-element.23) | copy-start | bytes 36868
  156.4 7.0 %copy-start.2 = (f32[3,256,256]{2,1,0:T(8,128)S(1)}, f32[3,256,256]{2,1,0:T(8,128)}, u32[]{:S(2)}) copy-start(f32[3,256,256]{2,1,0:T(8,128)} %get-tuple-element.21) | copy-start | bytes 2359300
  157.7 6.6 %copy-start.1 = (f32[3,256,256]{2,1,0:T(8,128)S(1)}, f32[3,256,256]{2,1,0:T(8,128)}, u32[]{:S(2)}) copy-start(f32[3,256,256]{2,1,0:T(8,128)} %get-tuple-element.22) | copy-start | bytes 2359300
where the time goes:
time: 168 us; the launch traced here: 165 us
  Pallas kernels  152 us (90%)
  local copies, waits for them, and re-layouts  10.3 us (6%)
  other arithmetic  1.76 us (1%)
    pallas_call x1, Pallas kernels, shards(): pl.pallas_call(functools.partial(block_kernel, cfg), out_shape=(jax.Shape...  152 us
    unnamed x12, local copies, waits for them, and re-layouts  4.85 us

commit v1 on v0

v1 whole, which is shorter than its diff:
```python
import functools
import types

import jax
import jax.numpy as jnp
from jax import lax
from jax.experimental import pallas as pl
from jax.experimental.pallas import tpu as pltpu
from jax.sharding import PartitionSpec as P

EPS = 1e-05
MASKED = -1e30
HEADS = 4
HD = 64
BF = jnp.bfloat16
F32 = jnp.float32
MESH = pl.DeviceIdType.MESH
VMEM_LIMIT = 60 * 1024 * 1024


def nn(a, b):
    return lax.dot_general(a, b, (((1,), (0,)), ((), ())), preferred_element_type=F32)


def nt(a, b):
    return lax.dot_general(a, b, (((1,), (1,)), ((), ())), preferred_element_type=F32)


def normalise(x):
    mean = jnp.mean(x, axis=-1, keepdims=True)
    centred = x - mean
    rstd = lax.rsqrt(jnp.mean(centred * centred, axis=-1, keepdims=True) + EPS)
    return centred * rstd, rstd


def norm_back(grad, gain, xhat, rstd):
    gl = grad * gain
    m1 = jnp.mean(gl, axis=-1, keepdims=True)
    m2 = jnp.mean(gl * xhat, axis=-1, keepdims=True)
    return rstd * (gl - m1 - xhat * m2)


def fold(x):
    return jnp.sum(x.reshape(x.shape[0] // 8, 8, x.shape[1]), axis=0)


def gelu_parts(x):
    c0 = 0.7978845608028654
    x2 = x * x
    t = jnp.tanh(c0 * (x + 0.044715 * (x2 * x)))
    half = 0.5 * (1.0 + t)
    slope = half + (0.5 * x) * (1.0 - t * t) * (c0 * (1.0 + (3 * 0.044715) * x2))
    return x * half, slope


def head_rows(x, h):
    own = x[h * HD:(h + 1) * HD]
    zero = jnp.zeros_like(own)
    return jnp.concatenate([own, zero] if h % 2 == 0 else [zero, own], axis=0)


def pair(h):
    return slice((h // 2) * 2 * HD, (h // 2 + 1) * 2 * HD)


def heads_apart(x):
    lane = lax.broadcasted_iota(jnp.int32, x.shape, 1)
    return jnp.concatenate(
        [jnp.where((lane >= h * HD) & (lane < (h + 1) * HD), x, jnp.zeros((), x.dtype)) for h in range(HEADS)], axis=0)


def wide(x, n):
    return jnp.concatenate([x] * (n // 128), axis=1)


class Share:
    def __init__(self, v, start, w, into):
        self.v, self.w = v, w
        self.cols = slice(start, start + w)
        self.start_lane = start
        self.r1, self.r2, self.r3, self.r4, self.send, self.recv = into
        self.Z, self.X = v.DP // 2, v.S // 2
        D = v.D
        self.k, self.x = lax.rem(v.me, 2), lax.div(v.me, 2)
        self.y, self.z = lax.rem(v.dp, 2), lax.div(v.dp, 2)
        self.h1, self.h2, self.h3 = D // 2, D // 4, D // 4 // self.Z
        self.b1 = self.k * self.h1
        self.b2 = self.b1 + self.y * self.h2
        self.b3 = self.b2 + self.z * self.h3
        self.wx = w // self.X

    def rows(self, base, n):
        return pl.ds(pl.multiple_of(base, 16), n)

    def lanes(self, x):
        return pl.ds(pl.multiple_of(self.start_lane + x * self.wx, 128), self.wx)

    def copies(self, i):
        v, Z, X = self.v, self.Z, self.X
        if i == 1 or i == 8:
            dev = (v.dp, v.me + 1 - 2 * self.k)
            if i == 1:
                return [(v.stage.at[self.rows((1 - self.k) * self.h1, self.h1), self.cols], self.r1, dev)]
            ref = v.gath.at[self.rows(self.b1, self.h1), self.cols]
            return [(ref, ref, dev)]
        if i == 2 or i == 7:
            dev = (v.dp + 1 - 2 * self.y, v.me)
            if i == 2:
                return [(v.stage.at[self.rows(self.b1 + (1 - self.y) * self.h2, self.h2), self.cols], self.r2, dev)]
            ref = v.gath.at[self.rows(self.b2, self.h2), self.cols]
            return [(ref, ref, dev)]
        out = []
        if i == 3 or i == 6:
            for j in range(1, Z):
                other = lax.rem(self.z + j, Z)
                dev = (other * 2 + self.y, v.me)
                if i == 3:
                    out.append((v.stage.at[self.rows(self.b2 + other * self.h3, self.h3), self.cols], self.r3.at[j - 1], dev))
                else:
                    ref = v.gath.at[self.rows(self.b3, self.h3), self.cols]
                    out.append((ref, ref, dev))
            return out
        for j in range(1, X):
            other = lax.rem(self.x + j, X)
            dev = (v.dp, other * 2 + self.k)
            if i == 4:
                out.append((v.stage.at[self.rows(self.b3, self.h3), self.lanes(other)], self.r4.at[j - 1], dev))
            else:
                ref = v.gath.at[self.rows(self.b3, self.h3), self.lanes(self.x)]
                out.append((ref, ref, dev))
        return out

    def made(self, i):
        return [pltpu.make_async_remote_copy(src_ref=s, dst_ref=d, send_sem=self.send.at[i - 1, j], recv_sem=self.recv.at[i - 1, j],
                                             device_id=dev, device_id_type=MESH)
                for j, (s, d, dev) in enumerate(self.copies(i))]

    def start(self, i):
        v = self.v
        if i == 1:
            there = self.rows((1 - self.k) * self.h1, self.h1)
            v.stage[there, self.cols] = v.dW[there, self.cols].astype(BF)
        for c in self.made(i):
            c.start()

    def finish(self, i):
        v = self.v
        for c in self.made(i):
            c.wait()
        if i == 1:
            here, n, got = self.rows(self.b1, self.h1), self.h1, [self.r1]
        elif i == 2:
            here, n, got = self.rows(self.b2, self.h2), self.h2, [self.r2]
        elif i == 3:
            here, n, got = self.rows(self.b3, self.h3), self.h3, [self.r3.at[j] for j in range(self.Z - 1)]
        elif i == 4:
            here = self.rows(self.b3, self.h3)
            total = v.dW[here, self.lanes(self.x)]
            for j in range(self.X - 1):
                total = total + self.r4[j].astype(F32)
            v.gath[here, self.lanes(self.x)] = total.astype(BF)
            return
        else:
            return
        total = v.dW[here, self.cols]
        for g in got:
            total = total + g[...].astype(F32)
        v.dW[here, self.cols] = total
        v.stage[here, self.cols] = total.astype(BF)

    def step(self, i):
        if i >= 1:
            self.finish(i)
        if i < 8:
            self.start(i + 1)


class SmallSum:
    def __init__(self, v):
        self.v = v

    def copies(self, i):
        v = self.v
        buf, n, me, send, recv = (v.vs_seq, v.S, v.me, v.vss, v.vsr) if i == 0 else (v.vs_dp, v.DP, v.dp, v.vds, v.vdr)
        out = []
        for k in range(1, n):
            other = lax.rem(me + k, n)
            out.append(pltpu.make_async_remote_copy(
                src_ref=buf.at[me], dst_ref=buf.at[me], send_sem=send.at[k - 1], recv_sem=recv.at[k - 1],
                device_id=(v.dp, other) if i == 0 else (other, v.me), device_id_type=MESH))
        return out

    def start(self, i):
        for c in self.copies(i):
            c.start()

    def finish(self, i):
        for c in self.copies(i):
            c.wait()
        v = self.v
        buf, n = (v.vs_seq, v.S) if i == 0 else (v.vs_dp, v.DP)
        total = buf[0]
        for s in range(1, n):
            total = total + buf[s]
        return total


def block_kernel(cfg, names, *refs):
    S, DP, R, L, D, FF, reduce_here = cfg
    W = 4 * D + 2 * FF
    v = types.SimpleNamespace(**dict(zip(names, refs, strict=True)))
    v.S, v.DP, v.R, v.L, v.D, v.FF, v.W, v.reduce_here = S, DP, R, L, D, FF, W, reduce_here
    v.me, v.dp = me, dp = lax.axis_index("seq"), lax.axis_index("dp")
    v.chip, v.core = chip, core = lax.div(me, 2), lax.rem(me, 2)
    X = S // 2
    v.mine = mine = pl.ds(pl.multiple_of(me * L, L), L)
    sizes = (S // 2, S) if S > 1 else (S,)

    def with_size(body):
        low = 0
        for n in sizes:
            pl.when((me >= low) & (me < n))(functools.partial(body, n))
            low = n

    @pl.loop(me + 1, S)
    def _(t):
        for a in range(2):
            for r in range(R):
                v.nall[a, r, pl.ds(pl.multiple_of(t * L, L), L)] = jnp.zeros((L, D), BF)

    barrier = pltpu.get_barrier_semaphore()
    for k in range(1, S):
        pl.semaphore_signal(barrier, inc=1, device_id=(dp, lax.rem(me + k, S)), device_id_type=MESH)
    peers = S - 1
    if reduce_here:
        for k in range(1, DP):
            pl.semaphore_signal(barrier, inc=1, device_id=(lax.rem(dp + k, DP), me), device_id_type=MESH)
        peers += DP - 1

    ln1g, ln1b = v.ln1g[...], v.ln1b[...]
    ln2g, ln2b = v.ln2g[...], v.ln2b[...]

    def block_of(a, r, t):
        return v.nall.at[a, r, pl.ds(pl.multiple_of(t * L, L), L)]

    def normed_copy(a, r, t, send_sem, dst):
        ref = block_of(a, r, t)
        return pltpu.make_async_remote_copy(
            src_ref=ref, dst_ref=ref, send_sem=send_sem, recv_sem=v.nrecv.at[a, r, t], device_id=(dp, dst), device_id_type=MESH)

    def to_chip(a, r, c):
        return normed_copy(a, r, me, v.nsend.at[a, r, c], 2 * c + core)

    def to_sibling(a, r):
        return normed_copy(a, r, me, v.nsend.at[a, r, X], me + 1 - 2 * core)

    def handed_on(a, r, c):
        return normed_copy(a, r, 2 * c + core, v.fsend.at[a, r, c], me + 1 - 2 * core)

    def each_send(a, r, action):
        @pl.loop(chip + 1, X)
        def _(c):
            action(to_chip(a, r, c))

        @pl.when(core == 0)
        def _():
            action(to_sibling(a, r))

    def first_norm(a, r):
        u = v.stream[r] + v.emb[r].astype(F32)
        v.stream[r] = u
        xhat, rstd = normalise(u)
        v.xh1[a, r] = xhat
        v.rs1[a, r] = jnp.broadcast_to(rstd, (L, 128))
        v.nall[a, r, mine] = (xhat * ln1g + ln1b).astype(BF)

    def announce(a, r):
        each_send(a, r, lambda c: c.start())

    def hand_on(a, r):
        @pl.loop(0, chip)
        def _(c):
            handed_on(a, r, c).wait_recv()
            handed_on(a, r, c).start()

    def gathered(a, r):
        @pl.loop(0, chip)
        def _(c):
            normed_copy(a, r, 2 * c + 1 - core, v.fsend.at[a, r, c], me).wait_recv()

        @pl.when(core == 1)
        def _():
            normed_copy(a, r, me - 1, v.nsend.at[a, r, X], me).wait_recv()

    @pl.loop(0, R)
    def _(r):
        v.stream[r] = v.hid[r].astype(F32)

    first_norm(0, 0)
    pl.semaphore_wait(barrier, peers)
    announce(0, 0)

    for k in range(3):
        v.wT[k] = v.wqkv[:, k * D:(k + 1) * D].T
    for k in range(2):
        v.bcol[k] = jnp.broadcast_to(v.qvb[k:k + 1, :], (128, D)).T
    v.vec[...] = jnp.zeros_like(v.vec)

    @pl.loop(1, R)
    def _(r):
        first_norm(0, r)
        announce(0, r)

    def forward_attention(a, r, bias, s_scr, nb):
        KB = nb * L
        length = v.lengths[r]
        rows = v.nall[a, r, 0:KB, :]
        keys = nn(rows, v.wqkv[:, D:2 * D]).astype(BF)
        VT = (nt(v.wT[2], rows) + wide(v.bcol[1], KB)).astype(BF)
        qT = v.qT[...]
        for t in range(nb):
            key_pos = t * L + lax.broadcasted_iota(jnp.int32, (L, L), 0)
            query_pos = me * L + lax.broadcasted_iota(jnp.int32, (L, L), 1)
            bias[t * L:(t + 1) * L] = jnp.where((key_pos <= query_pos) & (key_pos < length), 0.0, MASKED)
        tops = []
        for h in range(HEADS):
            s = nn(keys[:, pair(h)], head_rows(qT, h)) + bias[0:KB]
            s_scr[0:KB, h * L:(h + 1) * L] = s
            tops.append(jnp.max(jnp.max(s.reshape(KB // 8, 8, L), axis=0), axis=0, keepdims=True))
        for h in range(HEADS):
            hs = slice(h * HD, (h + 1) * HD)
            e = jnp.exp(s_scr[0:KB, h * L:(h + 1) * L] - tops[h])
            inv = 1.0 / jnp.sum(fold(e), axis=0, keepdims=True)
            low = e.astype(BF)
            v.e_scr[a, r, 0:KB, h * L:(h + 1) * L] = low
            v.linv[a, r, h] = jnp.broadcast_to(inv, (8, L))
            v.oT[a, r, hs] = (nn(VT[hs], low) * inv).astype(BF)

    def forward_all(bias, s_scr):
        hand_on(0, 0)

        @pl.loop(0, 2 * R)
        def _(n):
            a, r = lax.div(n, R), lax.rem(n, R)
            normed = v.nall[a, r, mine]
            qT = ((nt(v.wT[0], normed) + wide(v.bcol[0], L)) * (HD ** -0.5)).astype(BF)
            v.qn[a, r] = qT.T
            v.qT[...] = qT
            gathered(a, r)
            with_size(functools.partial(forward_attention, a, r, bias, s_scr))

            @pl.when(n < 2 * R - 1)
            def _():
                hand_on(lax.div(n + 1, R), lax.rem(n + 1, R))

            middle = v.stream[r] + (nn(v.oT[a, r].T, v.wout[...]) + v.bout[...])
            xhat, rstd = normalise(middle)
            v.xh2[a, r] = xhat
            v.rs2[a, r] = jnp.broadcast_to(rstd, (L, 128))
            normed2 = (xhat * ln2g + ln2b).astype(BF)
            v.n2T[a, r] = normed2.T
            hidden, slope = gelu_parts(nn(normed2, v.wup[...]) + v.bup[...])
            hidden = hidden.astype(BF)
            v.hidden[a, r] = hidden
            v.slope[a, r] = slope
            v.stream[r] = middle + (nn(hidden, v.wdn[...]) + v.bdn[...])

            @pl.when(a == 0)
            def _():
                first_norm(1, r)
                announce(1, r)

            @pl.when(a == 1)
            def _():
                v.y[r] = v.stream[r].astype(BF)
                v.gstream[r] = v.cot[r].astype(F32)

    VM = pltpu.VMEM
    pl.run_scoped(forward_all, VM((S * L, L), F32), VM((S * L, HEADS * L), F32))
    pl.run_scoped(functools.partial(backward, v, with_size), VM((R, D, L), BF), VM((R, L, FF), BF), VM((R, L, D), BF),
                  VM((R, L, 3 * D), BF), VM((D, W), F32), VM((S * L, HEADS * L), BF))

    for a in range(2):
        for r in range(R):
            each_send(a, r, lambda c: c.wait_send())

            @pl.loop(0, chip)
            def _(c):
                handed_on(a, r, c).wait_send()


def backward(v, with_size, gbT, gpre, ga_s, gqkv, dW, ds_s):
    S, DP, R, L, D, FF, W = v.S, v.DP, v.R, v.L, v.D, v.FF, v.W
    me, dp, mine = v.me, v.dp, v.mine
    v.dW = dW
    ln1g, ln2g = v.ln1g[...], v.ln2g[...]
    UP, DN, OW, QW = 0, FF, 2 * FF, 2 * FF + D
    V_LN1G, V_LN1B, V_QB, V_VB, V_OB, V_LN2G, V_LN2B, V_DB, V_UB = [D * k for k in range(9)]

    def part_copy(a, r, src, dst):
        return pltpu.make_async_remote_copy(
            src_ref=v.pg_out.at[a, r, dst], dst_ref=v.pg_in.at[a, r, src - 1], send_sem=v.psend.at[a, r, dst],
            recv_sem=v.precv.at[a, r, src], device_id=(dp, dst), device_id_type=MESH)

    def add_vec(start, terms):
        v.vec[:, start:start + terms.shape[1]] += fold(terms)

    def backward_mlp(a, r):
        g = v.gstream[r]
        gb = g.astype(BF)
        add_vec(V_DB, gb.astype(F32))
        gbT[r] = gb.T
        pre = (nt(gb, v.wdn[...]) * v.slope[a, r]).astype(BF)
        gpre[r] = pre
        add_vec(V_UB, pre.astype(F32))
        gn2 = nt(pre, v.wup[...])
        xhat = v.xh2[a, r]
        add_vec(V_LN2G, gn2 * xhat)
        add_vec(V_LN2B, gn2)
        gm = g + norm_back(gn2, ln2g, xhat, wide(v.rs2[a, r], D))
        v.gmid[r] = gm
        ga = gm.astype(BF)
        ga_s[r] = ga
        add_vec(V_OB, ga.astype(F32))

    def attention_core(a, r, nb):
        KB = nb * L
        gaT = nt(v.wout[...], ga_s[r]).astype(BF).astype(F32)
        oT = v.oT[a, r].astype(F32)
        scaled, deltas = [], []
        for h in range(HEADS):
            hs = slice(h * HD, (h + 1) * HD)
            part = gaT[hs] * v.linv[a, r, h, 0:1]
            scaled.append(part.astype(BF))
            deltas.append(jnp.sum(part * oT[hs], axis=0, keepdims=True))
        gaT_n = jnp.concatenate(scaled, axis=0)
        rows = v.nall[a, r, 0:KB, :]
        values = (nn(rows, v.wqkv[:, 2 * D:]) + v.qvb[1:2, :]).astype(BF)
        KT = nt(v.wT[1], rows).astype(BF)
        for h in range(HEADS):
            hl = slice(h * L, (h + 1) * L)
            gp = nn(values[:, pair(h)], head_rows(gaT_n, h))
            ds_s[0:KB, hl] = (v.e_scr[a, r, 0:KB, hl].astype(F32) * (gp - deltas[h])).astype(BF)
        gv = nn(v.e_scr[a, r, 0:KB, :], heads_apart(gaT_n.T))
        gk = nn(ds_s[0:KB, :], heads_apart(v.qn[a, r]))
        gkv = jnp.concatenate([gk, gv], axis=1).astype(BF)
        gqT = jnp.concatenate([nn(KT[h * HD:(h + 1) * HD], ds_s[0:KB, h * L:(h + 1) * L]) for h in range(HEADS)], axis=0)
        pg = nt(gkv, v.wqkv[:, D:]).astype(BF)
        for t in range(nb):
            @pl.when(t < me)
            def _():
                v.pg_out[a, r, t] = pg[t * L:(t + 1) * L]
                part_copy(a, r, me, t).start()

            @pl.when(t == me)
            def _():
                gqkv[r, :, D:] = gkv[t * L:(t + 1) * L]

        add_vec(V_VB, gkv[:, D:].astype(F32))
        dW[:, QW + D:QW + 3 * D] += nn(rows.T, gkv)
        gq = (gqT * (HD ** -0.5)).T.astype(BF)
        gqkv[r, :, :D] = gq
        add_vec(V_QB, gq.astype(F32))

    def backward_norm(a, r):
        gn = nt(gqkv[r], v.wqkv[...])

        def add(s, total):
            part_copy(a, r, s, me).wait_recv()
            return total + v.pg_in[a, r, s - 1].astype(F32)

        gn = lax.fori_loop(me + 1, S, add, gn)
        xhat = v.xh1[a, r]
        add_vec(V_LN1G, gn * xhat)
        add_vec(V_LN1B, gn)
        v.gstream[r] = v.gmid[r] + norm_back(gn, ln1g, xhat, wide(v.rs1[a, r], D))

    def put(first, start, value):
        if first:
            dW[:, start:start + value.shape[1]] = value
        else:
            dW[:, start:start + value.shape[1]] += value

    def weight_terms(a):
        first = a == 1
        put(first, UP, sum(nn(v.n2T[a, r], gpre[r]) for r in range(R)))
        put(first, DN, sum(nn(gbT[r], v.hidden[a, r]) for r in range(R)))
        put(first, OW, sum(nn(v.oT[a, r], ga_s[r]) for r in range(R)))

    def query_terms(a):
        put(a == 1, QW, sum(nn(v.nall[a, r, mine].T, gqkv[r, :, :D]) for r in range(R)))

    shares = []
    if v.reduce_here:
        into = lambda p: tuple(getattr(v, f"{n}_{p}") for n in ("r1", "r2", "r3", "r4", "ss", "sr"))
        shares = [Share(v, 0, 2 * FF + D, into(0)), Share(v, QW, 3 * D, into(1))]

    dW[:, QW + D:QW + 3 * D] = jnp.zeros((D, 2 * D), F32)
    for a in (1, 0):
        @pl.loop(0, R)
        def _(r):
            backward_mlp(a, r)

        weight_terms(a)

        @pl.loop(0, R)
        def _(r):
            with_size(functools.partial(attention_core, a, r))

        query_terms(a)

        @pl.loop(0, R)
        def _(r):
            backward_norm(a, r)
            if a == 1:
                v.g1[r] = v.gstream[r]
            else:
                g = v.gstream[r]
                v.ge[r] = g + v.g1[r]
                v.g1[r] = g

    sums = jnp.sum(v.vec[...], axis=0, keepdims=True)
    if v.reduce_here:
        for k in range(W // 128):
            v.vs_seq[me, k:k + 1, :] = sums[:, k * 128:(k + 1) * 128]
        small = SmallSum(v)
        small.start(0)
        for share in shares:
            share.start(1)
        v.vs_dp[dp] = small.finish(0)
        small.start(1)
        for i in range(1, 9):
            for share in shares:
                share.step(i)
            if i == 1:
                v.gv[...] = small.finish(1)
        out = pltpu.make_async_copy(v.gath, v.gw, v.out_sem)
        out.start()
        out.wait()
    else:
        out = pltpu.make_async_copy(v.gath if v.reduce_here else dW, v.gw, v.out_sem)
        out.start()
        out.wait()
        for k in range(W // 128):
            v.gv[k:k + 1, :] = sums[:, k * 128:(k + 1) * 128]

    for a in range(2):
        for r in range(R):
            @pl.loop(0, me)
            def _(dst):
                part_copy(a, r, me, dst).wait_send()


def finish_kernel(D, FF, names, *refs):
    v = types.SimpleNamespace(**dict(zip(names, refs, strict=True)))
    load = lambda i, src, dst: pltpu.make_async_copy(src, dst, v.sems.at[0, i])
    save = lambda i, src, dst: pltpu.make_async_copy(src, dst, v.sems.at[1, i])
    loads = [load(0, v.gw, v.gw_s), load(1, v.gv, v.gv_s), load(2, v.g1, v.g1_s), load(3, v.ge, v.ge_s), load(4, v.y, v.y_s)]
    for c in loads:
        c.start()
    saves = []

    def keep(src, dst):
        saves.append(save(len(saves), src, dst))
        saves[-1].start()

    loads[0].wait()
    v.wup_s[...] = v.gw_s[:, 0:FF].astype(F32)
    keep(v.wup_s, v.wup)
    v.wdn_s[...] = v.gw_s[:, FF:2 * FF].T.astype(F32)
    keep(v.wdn_s, v.wdn)
    v.wqkv_s[...] = v.gw_s[:, 2 * FF + D:].astype(F32)
    keep(v.wqkv_s, v.wqkv)
    v.wout_s[...] = v.gw_s[:, 2 * FF:2 * FF + D].astype(F32)
    keep(v.wout_s, v.wout)
    for c, src, dst in zip(loads[2:], (v.g1_s, v.ge_s, v.y_s), (v.g1_o, v.ge_o, v.y_o)):
        c.wait()
        keep(src, dst)
    loads[1].wait()
    n = D // 128
    at = 0
    for ref, size in ((v.ln1g, n), (v.ln1b, n), (v.qvb, 2 * n), (v.bout, n), (v.ln2g, n), (v.ln2b, n), (v.bdn, n),
                      (v.bup, FF // 128)):
        for k in range(size):
            row, col = divmod(k, ref.shape[1] // 128)
            ref[row:row + 1, col * 128:(col + 1) * 128] = v.gv_s[at + k:at + k + 1, :]
        at += size
    for c in saves:
        c.wait()


def solution(mesh):
    S, DP = mesh.shape["seq"], mesh.shape["dp"]

    def shards(hidden_in, embedding, lengths, cotangent, ln1_gain, ln1_bias, qkv_weight, qv_bias, out_weight, out_bias,
               ln2_gain, ln2_bias, up_weight, up_bias, down_weight, down_bias):
        L, R, D = hidden_in.shape
        FF = up_weight.shape[1]
        W = 4 * D + 2 * FF
        X, Z = max(S // 2, 1), max(DP // 2, 1)
        parts = (2 * FF + D, 3 * D)
        reduce_here = (S % 2 == 0 and DP % 2 == 0 and Z > 1 and X > 1 and (D // 4) % (16 * Z) == 0
                       and all(w % (128 * X) == 0 for w in parts))
        cfg = (S, DP, R, L, D, FF, reduce_here)
        VM = pltpu.VMEM
        DMA = pltpu.SemaphoreType.DMA
        scratch = dict(
            wT=VM((3, D, D), BF), bcol=VM((2, D, 128), F32), stream=VM((R, L, D), F32), gstream=VM((R, L, D), F32),
            gmid=VM((R, L, D), F32), nall=VM((2, R, S * L, D), BF), xh1=VM((2, R, L, D), F32), rs1=VM((2, R, L, 128), F32),
            xh2=VM((2, R, L, D), F32), rs2=VM((2, R, L, 128), F32), n2T=VM((2, R, D, L), BF), qT=VM((D, L), BF),
            qn=VM((2, R, L, D), BF), linv=VM((2, R, HEADS, 8, L), F32), oT=VM((2, R, D, L), BF),
            hidden=VM((2, R, L, FF), BF), slope=VM((2, R, L, FF), F32), e_scr=VM((2, R, S * L, HEADS * L), BF),
            pg_out=VM((2, R, S - 1, L, D), BF), pg_in=VM((2, R, S - 1, L, D), BF), vec=VM((8, W), F32),
            nsend=DMA((2, R, X + 1)), fsend=DMA((2, R, X)), nrecv=DMA((2, R, S)), psend=DMA((2, R, S)), precv=DMA((2, R, S)),
            out_sem=DMA)
        if reduce_here:
            most = max(Z, X) - 1
            scratch.update(
                stage=VM((D, W), BF), gath=VM((D, W), BF), vs_seq=VM((S, W // 128, 128), F32), vs_dp=VM((DP, W // 128, 128), F32),
                vss=DMA((S - 1,)), vsr=DMA((S - 1,)), vds=DMA((DP - 1,)), vdr=DMA((DP - 1,)))
            for p, w in enumerate(parts):
                scratch.update({
                    f"r1_{p}": VM((D // 2, w), BF), f"r2_{p}": VM((D // 4, w), BF), f"r3_{p}": VM((Z - 1, D // 4 // Z, w), BF),
                    f"r4_{p}": VM((X - 1, D // 4 // Z, w // X), BF), f"ss_{p}": DMA((8, most)), f"sr_{p}": DMA((8, most))})
        vm = pl.BlockSpec(memory_space=pltpu.VMEM)
        sm = pl.BlockSpec(memory_space=pltpu.SMEM)
        hbm = pl.BlockSpec(memory_space=pl.ANY)
        rows_first = lambda x: jnp.transpose(x, (1, 0, 2))
        line = lambda x: x.reshape(1, -1)
        ins = dict(
            hid=rows_first(hidden_in), emb=rows_first(embedding), cot=rows_first(cotangent), lengths=lengths, ln1g=line(ln1_gain),
            ln1b=line(ln1_bias), wqkv=qkv_weight, qvb=qv_bias, wout=out_weight, bout=line(out_bias), ln2g=line(ln2_gain),
            ln2b=line(ln2_bias), wup=up_weight, bup=line(up_bias), wdn=down_weight, bdn=line(down_bias))
        shape = jax.ShapeDtypeStruct
        outs = dict(
            y=shape((R, L, D), BF), g1=shape((R, L, D), F32), ge=shape((R, L, D), F32),
            gw=shape((D, W), BF if reduce_here else F32), gv=shape((W // 128, 128), F32))
        names = (*ins, *outs, *scratch)
        y, g1, ge, gw, gv = pl.pallas_call(
            functools.partial(block_kernel, cfg, names), out_shape=tuple(outs.values()),
            in_specs=[sm if n == "lengths" else vm for n in ins], out_specs=tuple(hbm if n == "gw" else vm for n in outs),
            scratch_shapes=list(scratch.values()),
            compiler_params=pltpu.CompilerParams(collective_id=0, has_side_effects=True, vmem_limit_bytes=VMEM_LIMIT),
        )(*ins.values())
        if not reduce_here:
            gw, gv = lax.psum((gw, gv), ("dp", "seq"))
        full = [shape((R, L, D), BF), shape((R, L, D), F32), shape((R, L, D), F32), shape((1, D), F32), shape((1, D), F32),
                shape((D, 3 * D), F32), shape((2, D), F32), shape((D, D), F32), shape((1, D), F32), shape((1, D), F32),
                shape((1, D), F32), shape((D, FF), F32), shape((1, FF), F32), shape((FF, D), F32), shape((1, D), F32)]
        ends = ["y_o", "g1_o", "ge_o", "ln1g", "ln1b", "wqkv", "qvb", "wout", "bout", "ln2g", "ln2b", "wup", "bup", "wdn", "bdn"]
        large = ("y_o", "g1_o", "ge_o", "wqkv", "wout", "wup", "wdn")
        temps = dict(
            y_s=VM((R, L, D), BF), g1_s=VM((R, L, D), F32), ge_s=VM((R, L, D), F32), gw_s=VM((D, W), gw.dtype),
            gv_s=VM((W // 128, 128), F32), wup_s=VM((D, FF), F32), wdn_s=VM((FF, D), F32), wqkv_s=VM((D, 3 * D), F32),
            wout_s=VM((D, D), F32), sems=DMA((2, 7)))
        res = pl.pallas_call(
            functools.partial(finish_kernel, D, FF, (*outs, *ends, *temps)), out_shape=full, in_specs=[hbm] * 5,
            out_specs=[hbm if n in large else vm for n in ends], scratch_shapes=list(temps.values()),
            compiler_params=pltpu.CompilerParams(vmem_limit_bytes=VMEM_LIMIT))(y, g1, ge, gw, gv)
        flat = (3, 4, 8, 9, 10, 12, 14)
        return tuple(rows_first(x) if i < 3 else x.reshape(-1) if i in flat else x for i, x in enumerate(res))

    token = P("seq", "dp", None)
    return jax.shard_map(
        shards, mesh=mesh, in_specs=(token, token, P("dp"), token) + (P(),) * 12, out_specs=(token,) * 3 + (P(),) * 12,
        check_vma=False)
```

time: 168 us -> 129 us (0.77)
  Pallas kernels: 152 us -> 126 us
  local copies, waits for them, and re-layouts: 10.3 us -> 0 us
  other arithmetic: 1.76 us -> 0 us
    pallas_call x1 -> x2, Pallas kernels: 152 us -> 126 us  [the longest x1 121 us: shards(): pl.pallas_call(functools.partial(block_kernel, cfg, names), out_shape=tup...]
    unnamed x12 -> x0, local copies, waits for them, and re-layouts: 4.85 us -> none
    slice x6 -> x0, local copies, waits for them, and re-layouts: 4.75 us -> none  [the longest x3 2.01 us: shards(): part = lambda k, n=1: gv[k * D:(k + n) * D]]
    convert_element_type x1 -> x0, other arithmetic: 1.76 us -> none  [shards(): gw = gw.astype(F32)]
where the time goes in v1:
time: 129 us; the launch traced here: 126 us
  Pallas kernels  126 us (98%)
    pallas_call x1, Pallas kernels, shards(): pl.pallas_call(functools.partial(block_kernel, cfg, names), out_shape=tup...  121 us
    pallas_call x1, Pallas kernels, shards(): pl.pallas_call(functools.partial(finish_kernel, D, FF, (*outs, *ends, *te...  4.66 us

profile of v1, /device:TPU:0, one launch (start us, length us, event | category | flops | bytes accessed | tf_op | source)
XLA Modules:
  0.0 126.5 jit_solution(8052632894217329990)
XLA Ops:
  0.7 121.0 %shard_map.271 = (bf16[3,256,256]{2,1,0:T(8,128)(2,1)}, f32[3,256,256]{2,1,0:T(8,128)}, f32[3,256,256]{2,1,0:T(8,128)}, bf16[256,3072]{1,0:T(8,128)(2,1)}, f32[24,128]{1,0:T(8,128)}) custom-call(bf16[3,256,256]{2,1,0:T(8,128)(2,1)} %bitcast.20, bf16[3,256,256]{2,1,0:T(8,128)(2,1)} %bitcast.21, bf16[3,256,256]{2,1,0:T(8,128)(2,1)} %bitcast.22, s32[3]{0:T(128)} %refs_3_.1, ...), custom_call_target="tpu_custom_call" | custom-call | tf_op jit(solution)/shard_map/pallas_call | solution.py:639
  121.6 4.7 %shard_map.272 = (bf16[3,256,256]{2,1,0:T(8,128)(2,1)}, f32[3,256,256]{2,1,0:T(8,128)}, f32[3,256,256]{2,1,0:T(8,128)}, f32[1,256]{1,0:T(1,128)}, f32[1,256]{1,0...) custom-call(bf16[3,256,256]{2,1,0:T(8,128)(2,1)} %get-tuple-element., ...), custom_call_target="tpu_custom_call" | custom-call | tf_op jit(solution)/shard_map/pallas_call | solution.py:656

commit v2 on v1

--- a/solution.py
+++ b/solution.py
@@ -75,59 +75,49 @@
 
 class Share:
     def __init__(self, v, start, w, into):
-        self.v, self.w = v, w
+        self.v, self.start_lane = v, start
         self.cols = slice(start, start + w)
-        self.start_lane = start
-        self.r1, self.r2, self.r3, self.r4, self.send, self.recv = into
-        self.Z, self.X = v.DP // 2, v.S // 2
-        D = v.D
-        self.k, self.x = lax.rem(v.me, 2), lax.div(v.me, 2)
-        self.y, self.z = lax.rem(v.dp, 2), lax.div(v.dp, 2)
-        self.h1, self.h2, self.h3 = D // 2, D // 4, D // 4 // self.Z
-        self.b1 = self.k * self.h1
-        self.b2 = self.b1 + self.y * self.h2
-        self.b3 = self.b2 + self.z * self.h3
-        self.wx = w // self.X
+        self.r1, self.r2, self.r3, self.send, self.recv = into
+        self.n2, self.n3 = v.S, v.DP // 2
+        self.h1 = v.D // 2
+        self.h2 = self.h1 // self.n2
+        self.groups = self.h2 // 16
+        self.w3 = w * self.groups // self.n3
+        self.b1 = v.core * self.h1
+        self.b2 = self.b1 + v.spot2 * self.h2
 
     def rows(self, base, n):
         return pl.ds(pl.multiple_of(base, 16), n)
 
-    def lanes(self, x):
-        return pl.ds(pl.multiple_of(self.start_lane + x * self.wx, 128), self.wx)
+    def chunk(self, z):
+        row, lane = lax.rem(z, self.groups), lax.div(z, self.groups)
+        return self.rows(self.b2 + row * 16, 16), pl.ds(pl.multiple_of(self.start_lane + lane * self.w3, 128), self.w3)
 
     def copies(self, i):
-        v, Z, X = self.v, self.Z, self.X
-        if i == 1 or i == 8:
-            dev = (v.dp, v.me + 1 - 2 * self.k)
-            if i == 1:
-                return [(v.stage.at[self.rows((1 - self.k) * self.h1, self.h1), self.cols], self.r1, dev)]
+        v = self.v
+        if i == 1:
+            return [(v.stage.at[self.rows((1 - v.core) * self.h1, self.h1), self.cols], self.r1, v.sibling)]
+        if i == 6:
             ref = v.gath.at[self.rows(self.b1, self.h1), self.cols]
-            return [(ref, ref, dev)]
-        if i == 2 or i == 7:
-            dev = (v.dp + 1 - 2 * self.y, v.me)
-            if i == 2:
-                return [(v.stage.at[self.rows(self.b1 + (1 - self.y) * self.h2, self.h2), self.cols], self.r2, dev)]
-            ref = v.gath.at[self.rows(self.b2, self.h2), self.cols]
-            return [(ref, ref, dev)]
+            return [(ref, ref, v.sibling)]
         out = []
-        if i == 3 or i == 6:
-            for j in range(1, Z):
-                other = lax.rem(self.z + j, Z)
-                dev = (other * 2 + self.y, v.me)
-                if i == 3:
-                    out.append((v.stage.at[self.rows(self.b2 + other * self.h3, self.h3), self.cols], self.r3.at[j - 1], dev))
+        if i in (2, 5):
+            for j in range(1, self.n2):
+                other = lax.rem(v.spot2 + j, self.n2)
+                if i == 2:
+                    src = v.stage.at[self.rows(self.b1 + other * self.h2, self.h2), self.cols]
+                    out.append((src, self.r2.at[j - 1], v.in_plane(other)))
                 else:
-                    ref = v.gath.at[self.rows(self.b3, self.h3), self.cols]
-                    out.append((ref, ref, dev))
+                    ref = v.gath.at[self.rows(self.b2, self.h2), self.cols]
+                    out.append((ref, ref, v.in_plane(other)))
             return out
-        for j in range(1, X):
-            other = lax.rem(self.x + j, X)
-            dev = (v.dp, other * 2 + self.k)
-            if i == 4:
-                out.append((v.stage.at[self.rows(self.b3, self.h3), self.lanes(other)], self.r4.at[j - 1], dev))
+        for j in range(1, self.n3):
+            other = lax.rem(v.spot3 + j, self.n3)
+            if i == 3:
+                out.append((v.stage.at[self.chunk(other)], self.r3.at[j - 1], v.across(other)))
             else:
-                ref = v.gath.at[self.rows(self.b3, self.h3), self.lanes(self.x)]
-                out.append((ref, ref, dev))
+                ref = v.gath.at[self.chunk(v.spot3)]
+                out.append((ref, ref, v.across(other)))
         return out
 
     def made(self, i):
@@ -138,7 +128,7 @@
     def start(self, i):
         v = self.v
         if i == 1:
-            there = self.rows((1 - self.k) * self.h1, self.h1)
+            there = self.rows((1 - v.core) * self.h1, self.h1)
             v.stage[there, self.cols] = v.dW[there, self.cols].astype(BF)
         for c in self.made(i):
             c.start()
@@ -147,62 +137,62 @@
         v = self.v
         for c in self.made(i):
             c.wait()
+        if i > 3:
+            return
         if i == 1:
-            here, n, got = self.rows(self.b1, self.h1), self.h1, [self.r1]
+            at, got = (self.rows(self.b1, self.h1), self.cols), [self.r1]
         elif i == 2:
-            here, n, got = self.rows(self.b2, self.h2), self.h2, [self.r2]
-        elif i == 3:
-            here, n, got = self.rows(self.b3, self.h3), self.h3, [self.r3.at[j] for j in range(self.Z - 1)]
-        elif i == 4:
-            here = self.rows(self.b3, self.h3)
-            total = v.dW[here, self.lanes(self.x)]
-            for j in range(self.X - 1):
-                total = total + self.r4[j].astype(F32)
-            v.gath[here, self.lanes(self.x)] = total.astype(BF)
-            return
+            at, got = (self.rows(self.b2, self.h2), self.cols), [self.r2.at[j] for j in range(self.n2 - 1)]
         else:
-            return
-        total = v.dW[here, self.cols]
+            at, got = self.chunk(v.spot3), [self.r3.at[j] for j in range(self.n3 - 1)]
+        total = v.dW[at]
         for g in got:
             total = total + g[...].astype(F32)
-        v.dW[here, self.cols] = total
-        v.stage[here, self.cols] = total.astype(BF)
+        if i == 3:
+            v.gath[at] = total.astype(BF)
+        else:
+            v.dW[at] = total
+            v.stage[at] = total.astype(BF)
 
     def step(self, i):
-        if i >= 1:
-            self.finish(i)
-        if i < 8:
+        self.finish(i)
+        if i < 6:
             self.start(i + 1)
 
 
 class SmallSum:
     def __init__(self, v):
         self.v = v
+        self.stages = [(v.vs1, v.core, 2, lambda other: v.sibling, v.vss1, v.vsr1),
+                       (v.vs2, v.spot2, v.S, v.in_plane, v.vss2, v.vsr2), (v.vs3, v.spot3, v.DP // 2, v.across, v.vss3, v.vsr3)]
 
     def copies(self, i):
-        v = self.v
-        buf, n, me, send, recv = (v.vs_seq, v.S, v.me, v.vss, v.vsr) if i == 0 else (v.vs_dp, v.DP, v.dp, v.vds, v.vdr)
-        out = []
-        for k in range(1, n):
-            other = lax.rem(me + k, n)
-            out.append(pltpu.make_async_remote_copy(
-                src_ref=buf.at[me], dst_ref=buf.at[me], send_sem=send.at[k - 1], recv_sem=recv.at[k - 1],
-                device_id=(v.dp, other) if i == 0 else (other, v.me), device_id_type=MESH))
-        return out
-
-    def start(self, i):
+        buf, spot, n, device, send, recv = self.stages[i]
+        return [pltpu.make_async_remote_copy(
+            src_ref=buf.at[spot], dst_ref=buf.at[spot], send_sem=send.at[k - 1], recv_sem=recv.at[k - 1],
+            device_id=device(lax.rem(spot + k, n)), device_id_type=MESH) for k in range(1, n)]
+
+    def start(self, i, value):
+        buf, spot = self.stages[i][:2]
+        buf[spot] = value
         for c in self.copies(i):
             c.start()
 
     def finish(self, i):
         for c in self.copies(i):
             c.wait()
-        v = self.v
-        buf, n = (v.vs_seq, v.S) if i == 0 else (v.vs_dp, v.DP)
+        buf, n = self.stages[i][0], self.stages[i][2]
         total = buf[0]
         for s in range(1, n):
             total = total + buf[s]
         return total
+
+
+def out_copy(v, which, src, dst, r):
+    return pltpu.make_async_copy(src.at[r], dst.at[r], v.out_sems.at[which, r])
+
+
+LOADS = ("hid", "emb", "ln1g", "ln1b", "wqkv", "qvb", "wup", "wdn", "wout", "bout", "ln2g", "ln2b", "bup", "bdn", "cot")
 
 
 def block_kernel(cfg, names, *refs):
@@ -212,9 +202,10 @@
     v.S, v.DP, v.R, v.L, v.D, v.FF, v.W, v.reduce_here = S, DP, R, L, D, FF, W, reduce_here
     v.me, v.dp = me, dp = lax.axis_index("seq"), lax.axis_index("dp")
     v.chip, v.core = chip, core = lax.div(me, 2), lax.rem(me, 2)
-    X = S // 2
+    X = v.X = S // 2
     v.mine = mine = pl.ds(pl.multiple_of(me * L, L), L)
-    sizes = (S // 2, S) if S > 1 else (S,)
+    v.sibling = (dp, me + 1 - 2 * core)
+    sizes = (S // 2, S)
 
     def with_size(body):
         low = 0
@@ -222,23 +213,27 @@
             pl.when((me >= low) & (me < n))(functools.partial(body, n))
             low = n
 
-    @pl.loop(me + 1, S)
-    def _(t):
-        for a in range(2):
-            for r in range(R):
-                v.nall[a, r, pl.ds(pl.multiple_of(t * L, L), L)] = jnp.zeros((L, D), BF)
-
     barrier = pltpu.get_barrier_semaphore()
-    for k in range(1, S):
-        pl.semaphore_signal(barrier, inc=1, device_id=(dp, lax.rem(me + k, S)), device_id_type=MESH)
-    peers = S - 1
+    peers = [v.sibling] + [(dp, lax.rem(me + 2 * k, S)) for k in range(1, X)]
     if reduce_here:
-        for k in range(1, DP):
-            pl.semaphore_signal(barrier, inc=1, device_id=(lax.rem(dp + k, DP), me), device_id_type=MESH)
-        peers += DP - 1
-
-    ln1g, ln1b = v.ln1g[...], v.ln1b[...]
-    ln2g, ln2b = v.ln2g[...], v.ln2b[...]
+        v.spot2, v.spot3 = chip * 2 + lax.rem(dp, 2), lax.div(dp, 2)
+        v.in_plane = lambda n: (lax.div(dp, 2) * 2 + lax.rem(n, 2), lax.div(n, 2) * 2 + core)
+        v.across = lambda n: (n * 2 + lax.rem(dp, 2), me)
+        peers += [(dp + 1 - 2 * lax.rem(dp, 2), lax.rem(me + 2 * k, S)) for k in range(X)]
+        peers += [v.across(lax.rem(v.spot3 + k, DP // 2)) for k in range(1, DP // 2)]
+    for peer in peers:
+        pl.semaphore_signal(barrier, inc=1, device_id=peer, device_id_type=MESH)
+
+    brought = {}
+    for k, name in enumerate(LOADS):
+        brought[name] = pltpu.make_async_copy(getattr(v, name + "_in"), getattr(v, name), v.in_sem.at[k])
+        brought[name].start()
+
+    def need(*which):
+        for name in which:
+            brought.pop(name).wait()
+
+    v.need = need
 
     def block_of(a, r, t):
         return v.nall.at[a, r, pl.ds(pl.multiple_of(t * L, L), L)]
@@ -292,31 +287,45 @@
         def _():
             normed_copy(a, r, me - 1, v.nsend.at[a, r, X], me).wait_recv()
 
+    @pl.loop(me + 1, S)
+    def _(t):
+        for a in range(2):
+            for r in range(R):
+                v.nall[a, r, pl.ds(pl.multiple_of(t * L, L), L)] = jnp.zeros((L, D), BF)
+
+    v.vec[...] = jnp.zeros_like(v.vec)
+    need("hid", "emb", "ln1g", "ln1b")
+    ln1g, ln1b = v.ln1g[...], v.ln1b[...]
+
     @pl.loop(0, R)
     def _(r):
         v.stream[r] = v.hid[r].astype(F32)
-
-    first_norm(0, 0)
-    pl.semaphore_wait(barrier, peers)
-    announce(0, 0)
-
+        first_norm(0, r)
+
+    need("wqkv", "qvb")
     for k in range(3):
-        v.wT[k] = v.wqkv[:, k * D:(k + 1) * D].T
+        v.wT[k * D:(k + 1) * D] = v.wqkv[:, k * D:(k + 1) * D].T
     for k in range(2):
         v.bcol[k] = jnp.broadcast_to(v.qvb[k:k + 1, :], (128, D)).T
-    v.vec[...] = jnp.zeros_like(v.vec)
-
-    @pl.loop(1, R)
-    def _(r):
-        first_norm(0, r)
+    need("wup", "wdn")
+    for k in range(FF // D):
+        ks = slice(k * D, (k + 1) * D)
+        v.wupT[ks] = v.wup[:, ks].T
+        v.wdnT[:, ks] = v.wdn[ks].T
+
+    pl.semaphore_wait(barrier, len(peers))
+    for r in range(R):
         announce(0, r)
+
+    need("wout", "bout", "ln2g", "ln2b", "bup", "bdn", "cot")
+    ln2g, ln2b = v.ln2g[...], v.ln2b[...]
 
     def forward_attention(a, r, bias, s_scr, nb):
         KB = nb * L
         length = v.lengths[r]
         rows = v.nall[a, r, 0:KB, :]
         keys = nn(rows, v.wqkv[:, D:2 * D]).astype(BF)
-        VT = (nt(v.wT[2], rows) + wide(v.bcol[1], KB)).astype(BF)
+        VT = (nt(v.wT[2 * D:], rows) + wide(v.bcol[1], KB)).astype(BF)
         qT = v.qT[...]
         for t in range(nb):
             key_pos = t * L + lax.broadcasted_iota(jnp.int32, (L, L), 0)
@@ -343,7 +352,7 @@
         def _(n):
             a, r = lax.div(n, R), lax.rem(n, R)
             normed = v.nall[a, r, mine]
-            qT = ((nt(v.wT[0], normed) + wide(v.bcol[0], L)) * (HD ** -0.5)).astype(BF)
+            qT = ((nt(v.wT[:D], normed) + wide(v.bcol[0], L)) * (HD ** -0.5)).astype(BF)
             v.qn[a, r] = qT.T
             v.qT[...] = qT
             gathered(a, r)
@@ -372,13 +381,14 @@
 
             @pl.when(a == 1)
             def _():
-                v.y[r] = v.stream[r].astype(BF)
+                v.hid[r] = v.stream[r].astype(BF)
                 v.gstream[r] = v.cot[r].astype(F32)
+                out_copy(v, 0, v.hid, v.y, r).start()
 
     VM = pltpu.VMEM
     pl.run_scoped(forward_all, VM((S * L, L), F32), VM((S * L, HEADS * L), F32))
     pl.run_scoped(functools.partial(backward, v, with_size), VM((R, D, L), BF), VM((R, L, FF), BF), VM((R, L, D), BF),
-                  VM((R, L, 3 * D), BF), VM((D, W), F32), VM((S * L, HEADS * L), BF))
+                  VM((R, L, 3 * D), BF), VM((D, W), F32), VM((L, D), F32))
 
     for a in range(2):
         for r in range(R):
@@ -389,7 +399,7 @@
                 handed_on(a, r, c).wait_send()
 
 
-def backward(v, with_size, gbT, gpre, ga_s, gqkv, dW, ds_s):
+def backward(v, with_size, gbT, gpre, ga_s, gqkv, dW, gns):
     S, DP, R, L, D, FF, W = v.S, v.DP, v.R, v.L, v.D, v.FF, v.W
     me, dp, mine = v.me, v.dp, v.mine
     v.dW = dW
@@ -397,10 +407,29 @@
     UP, DN, OW, QW = 0, FF, 2 * FF, 2 * FF + D
     V_LN1G, V_LN1B, V_QB, V_VB, V_OB, V_LN2G, V_LN2B, V_DB, V_UB = [D * k for k in range(9)]
 
+    X, chip, core = v.X, v.chip, v.core
+
+    def pair_copy(a, r, c):
+        return pltpu.make_async_remote_copy(
+            src_ref=v.pair_out.at[a, r, c], dst_ref=v.pair_in.at[a, r, c], send_sem=v.psend.at[0, a, r, c],
+            recv_sem=v.precv.at[0, a, r, c], device_id=v.sibling, device_id_type=MESH)
+
     def part_copy(a, r, src, dst):
         return pltpu.make_async_remote_copy(
-            src_ref=v.pg_out.at[a, r, dst], dst_ref=v.pg_in.at[a, r, src - 1], send_sem=v.psend.at[a, r, dst],
-            recv_sem=v.precv.at[a, r, src], device_id=(dp, dst), device_id_type=MESH)
+            src_ref=v.part_out.at[a, r, dst], dst_ref=v.part_in.at[a, r, src - 1], send_sem=v.psend.at[1, a, r, dst],
+            recv_sem=v.precv.at[1, a, r, src], device_id=(dp, 2 * dst + core), device_id_type=MESH)
+
+    def near_copy(a, r):
+        return pltpu.make_async_remote_copy(
+            src_ref=v.near_out.at[a, r], dst_ref=v.near_in.at[a, r], send_sem=v.nearsem.at[0, a, r],
+            recv_sem=v.nearsem.at[1, a, r], device_id=v.sibling, device_id_type=MESH)
+
+    def pass_on(a, r):
+        @pl.loop(0, chip)
+        def _(c):
+            pair_copy(a, r, c).wait_recv()
+            v.part_out[a, r, c] = (v.keep[r, c] + v.pair_in[a, r, c].astype(F32)).astype(BF)
+            part_copy(a, r, chip, c).start()
 
     def add_vec(start, terms):
         v.vec[:, start:start + terms.shape[1]] += fold(terms)
@@ -410,10 +439,10 @@
         gb = g.astype(BF)
         add_vec(V_DB, gb.astype(F32))
         gbT[r] = gb.T
-        pre = (nt(gb, v.wdn[...]) * v.slope[a, r]).astype(BF)
+        pre = (nn(gb, v.wdnT[...]) * v.slope[a, r]).astype(BF)
         gpre[r] = pre
         add_vec(V_UB, pre.astype(F32))
-        gn2 = nt(pre, v.wup[...])
+        gn2 = nn(pre, v.wupT[...])
         xhat = v.xh2[a, r]
         add_vec(V_LN2G, gn2 * xhat)
         add_vec(V_LN2B, gn2)
@@ -423,7 +452,7 @@
         ga_s[r] = ga
         add_vec(V_OB, ga.astype(F32))
 
-    def attention_core(a, r, nb):
+    def attention_core(a, r, tick, nb):
         KB = nb * L
         gaT = nt(v.wout[...], ga_s[r]).astype(BF).astype(F32)
         oT = v.oT[a, r].astype(F32)
@@ -436,21 +465,34 @@
         gaT_n = jnp.concatenate(scaled, axis=0)
         rows = v.nall[a, r, 0:KB, :]
         values = (nn(rows, v.wqkv[:, 2 * D:]) + v.qvb[1:2, :]).astype(BF)
-        KT = nt(v.wT[1], rows).astype(BF)
+        KT = nt(v.wT[D:2 * D], rows).astype(BF)
+        gv = nn(v.e_scr[a, r, 0:KB, :], heads_apart(gaT_n.T))
         for h in range(HEADS):
             hl = slice(h * L, (h + 1) * L)
             gp = nn(values[:, pair(h)], head_rows(gaT_n, h))
-            ds_s[0:KB, hl] = (v.e_scr[a, r, 0:KB, hl].astype(F32) * (gp - deltas[h])).astype(BF)
-        gv = nn(v.e_scr[a, r, 0:KB, :], heads_apart(gaT_n.T))
-        gk = nn(ds_s[0:KB, :], heads_apart(v.qn[a, r]))
+            v.e_scr[a, r, 0:KB, hl] = (v.e_scr[a, r, 0:KB, hl].astype(F32) * (gp - deltas[h])).astype(BF)
+        tick()
+        gk = nn(v.e_scr[a, r, 0:KB, :], heads_apart(v.qn[a, r]))
         gkv = jnp.concatenate([gk, gv], axis=1).astype(BF)
-        gqT = jnp.concatenate([nn(KT[h * HD:(h + 1) * HD], ds_s[0:KB, h * L:(h + 1) * L]) for h in range(HEADS)], axis=0)
-        pg = nt(gkv, v.wqkv[:, D:]).astype(BF)
+        gqT = jnp.concatenate([nn(KT[h * HD:(h + 1) * HD], v.e_scr[a, r, 0:KB, h * L:(h + 1) * L]) for h in range(HEADS)], axis=0)
+        pg = nn(gkv, v.wT[D:])
         for t in range(nb):
-            @pl.when(t < me)
-            def _():
-                v.pg_out[a, r, t] = pg[t * L:(t + 1) * L]
-                part_copy(a, r, me, t).start()
+            block = pg[t * L:(t + 1) * L]
+            if t // 2 < nb // 2 - 1:
+                @pl.when((t // 2 < chip) & (t % 2 == core))
+                def _():
+                    v.keep[r, t // 2] = block
+
+                @pl.when((t // 2 < chip) & (t % 2 != core))
+                def _():
+                    v.pair_out[a, r, t // 2] = block.astype(BF)
+                    pair_copy(a, r, t // 2).start()
+
+            if t % 2 == 0:
+                @pl.when(t == me - 1)
+                def _():
+                    v.near_out[a, r] = block.astype(BF)
+                    near_copy(a, r).start()
 
             @pl.when(t == me)
             def _():
@@ -463,13 +505,19 @@
         add_vec(V_QB, gq.astype(F32))
 
     def backward_norm(a, r):
-        gn = nt(gqkv[r], v.wqkv[...])
-
-        def add(s, total):
-            part_copy(a, r, s, me).wait_recv()
-            return total + v.pg_in[a, r, s - 1].astype(F32)
-
-        gn = lax.fori_loop(me + 1, S, add, gn)
+        gns[...] = nn(gqkv[r], v.wT[...])
+
+        @pl.when(core == 0)
+        def _():
+            near_copy(a, r).wait_recv()
+            gns[...] += v.near_in[a, r].astype(F32)
+
+        @pl.loop(chip + 1, X)
+        def _(c):
+            part_copy(a, r, c, chip).wait_recv()
+            gns[...] += v.part_in[a, r, c - 1].astype(F32)
+
+        gn = gns[...]
         xhat = v.xh1[a, r]
         add_vec(V_LN1G, gn * xhat)
         add_vec(V_LN1B, gn)
@@ -481,74 +529,139 @@
         else:
             dW[:, start:start + value.shape[1]] += value
 
-    def weight_terms(a):
-        first = a == 1
-        put(first, UP, sum(nn(v.n2T[a, r], gpre[r]) for r in range(R)))
-        put(first, DN, sum(nn(gbT[r], v.hidden[a, r]) for r in range(R)))
-        put(first, OW, sum(nn(v.oT[a, r], ga_s[r]) for r in range(R)))
+    def weight_terms(a, rows, which):
+        first = a == 1 and rows[0] == 0
+        if "up" in which:
+            put(first, UP, sum(nn(v.n2T[a, r], gpre[r]) for r in rows))
+        if "down" in which:
+            put(first, DN, sum(nn(gbT[r], v.hidden[a, r]) for r in rows))
+            put(first, OW, sum(nn(v.oT[a, r], ga_s[r]) for r in rows))
 
     def query_terms(a):
         put(a == 1, QW, sum(nn(v.nall[a, r, mine].T, gqkv[r, :, :D]) for r in range(R)))
 
-    shares = []
-    if v.reduce_here:
-        into = lambda p: tuple(getattr(v, f"{n}_{p}") for n in ("r1", "r2", "r3", "r4", "ss", "sr"))
-        shares = [Share(v, 0, 2 * FF + D, into(0)), Share(v, QW, 3 * D, into(1))]
-
+    every, early, last = tuple(range(R)), tuple(range(R - 1)), (R - 1,)
     dW[:, QW + D:QW + 3 * D] = jnp.zeros((D, 2 * D), F32)
-    for a in (1, 0):
-        @pl.loop(0, R)
-        def _(r):
-            backward_mlp(a, r)
-
-        weight_terms(a)
-
-        @pl.loop(0, R)
-        def _(r):
-            with_size(functools.partial(attention_core, a, r))
-
-        query_terms(a)
-
-        @pl.loop(0, R)
-        def _(r):
-            backward_norm(a, r)
-            if a == 1:
-                v.g1[r] = v.gstream[r]
-            else:
-                g = v.gstream[r]
-                v.ge[r] = g + v.g1[r]
-                v.g1[r] = g
-
-    sums = jnp.sum(v.vec[...], axis=0, keepdims=True)
-    if v.reduce_here:
-        for k in range(W // 128):
-            v.vs_seq[me, k:k + 1, :] = sums[:, k * 128:(k + 1) * 128]
+    reducing = v.reduce_here
+    if reducing:
+        into = lambda p: tuple(getattr(v, f"{n}_{p}") for n in ("r1", "r2", "r3", "ss", "sr"))
+        up, down, qkv = (Share(v, start, w, into(p)) for p, (start, w) in enumerate(((UP, FF), (DN, FF + D), (QW, 3 * D))))
         small = SmallSum(v)
-        small.start(0)
-        for share in shares:
-            share.start(1)
-        v.vs_dp[dp] = small.finish(0)
-        small.start(1)
-        for i in range(1, 9):
-            for share in shares:
-                share.step(i)
-            if i == 1:
-                v.gv[...] = small.finish(1)
-        out = pltpu.make_async_copy(v.gath, v.gw, v.out_sem)
+
+    def nothing():
+        pass
+
+    def attention(a, r, tick):
+        with_size(functools.partial(attention_core, a, r, tick if reducing else nothing))
+
+    @pl.loop(0, R)
+    def _(r):
+        backward_mlp(1, r)
+
+    weight_terms(1, every, ("up", "down"))
+
+    @pl.loop(0, R)
+    def _(r):
+        attention(1, r, nothing)
+
+        @pl.when(r > 0)
+        def _():
+            pass_on(1, r - 1)
+
+    query_terms(1)
+    pass_on(1, R - 1)
+
+    def between(r):
+        backward_norm(1, r)
+        v.stream[r] = v.gstream[r]
+        backward_mlp(0, r)
+
+    pl.loop(0, R - 1)(between)
+    if early:
+        weight_terms(0, early, ("up", "down"))
+    between(R - 1)
+    weight_terms(0, last, ("up",))
+    if reducing:
+        up.start(1)
+    weight_terms(0, last, ("down",))
+    if reducing:
+        down.start(1)
+
+    def tick_first():
+        up.step(1)
+        down.step(1)
+
+    def tick_last():
+        up.step(2)
+
+    for r in range(R):
+        attention(0, r, tick_first if r == 0 else tick_last if r == R - 1 else nothing)
+        if r > 0:
+            pass_on(0, r - 1)
+    if reducing:
+        down.step(2)
+    query_terms(0)
+    if reducing:
+        qkv.start(1)
+    pass_on(0, R - 1)
+
+    def final(r):
+        backward_norm(0, r)
+        v.gmid[r] = v.gstream[r] + v.stream[r]
+        out_copy(v, 1, v.gstream, v.g1, r).start()
+        out_copy(v, 2, v.gmid, v.ge, r).start()
+
+    def small_lines():
+        sums = jnp.sum(v.vec[...], axis=0, keepdims=True)
+        return jnp.concatenate([sums[:, k * 128:(k + 1) * 128] for k in range(W // 128)], axis=0)
+
+    if reducing:
+        qkv.step(1)
+        pl.loop(0, R - 1)(final)
+        up.step(3)
+        down.step(3)
+        final(R - 1)
+        small.start(0, small_lines())
+        qkv.step(2)
+        up.step(4)
+        small.start(1, small.finish(0))
+        down.step(4)
+        qkv.step(3)
+        small.start(2, small.finish(1))
+        up.step(5)
+        down.step(5)
+        v.gv[...] = small.finish(2)
+        qkv.step(4)
+        up.finish(6)
+        down.finish(6)
+        gath_copy = lambda k, cols: pltpu.make_async_copy(v.gath.at[:, cols], v.gw.at[:, cols], v.gw_sem.at[k])
+        first_out, second_out = gath_copy(0, slice(0, QW)), gath_copy(1, slice(QW, W))
+        first_out.start()
+        qkv.step(5)
+        qkv.finish(6)
+        second_out.start()
+        first_out.wait()
+        second_out.wait()
+    else:
+        pl.loop(0, R)(final)
+        out = pltpu.make_async_copy(v.gath if v.reduce_here else dW, v.gw, v.gw_sem.at[0])
         out.start()
         out.wait()
-    else:
-        out = pltpu.make_async_copy(v.gath if v.reduce_here else dW, v.gw, v.out_sem)
-        out.start()
-        out.wait()
-        for k in range(W // 128):
-            v.gv[k:k + 1, :] = sums[:, k * 128:(k + 1) * 128]
-
-    for a in range(2):
-        for r in range(R):
-            @pl.loop(0, me)
-            def _(dst):
-                part_copy(a, r, me, dst).wait_send()
+        v.gv[...] = small_lines()
+
+    for r in range(R):
+        out_copy(v, 0, v.hid, v.y, r).wait()
+        out_copy(v, 1, v.gstream, v.g1, r).wait()
+        out_copy(v, 2, v.gmid, v.ge, r).wait()
+        for a in range(2):
+            @pl.loop(0, chip)
+            def _(c):
+                pair_copy(a, r, c).wait_send()
+                part_copy(a, r, chip, c).wait_send()
+
+            @pl.when(core == 1)
+            def _():
+                near_copy(a, r).wait_send()
 
 
 def finish_kernel(D, FF, names, *refs):
@@ -597,31 +710,37 @@
         L, R, D = hidden_in.shape
         FF = up_weight.shape[1]
         W = 4 * D + 2 * FF
-        X, Z = max(S // 2, 1), max(DP // 2, 1)
-        parts = (2 * FF + D, 3 * D)
-        reduce_here = (S % 2 == 0 and DP % 2 == 0 and Z > 1 and X > 1 and (D // 4) % (16 * Z) == 0
-                       and all(w % (128 * X) == 0 for w in parts))
+        X, Z = S // 2, DP // 2
+        parts = (FF, FF + D, 3 * D)
+        h2 = D // 2 // S
+        groups = max(h2 // 16, 1)
+        reduce_here = (DP % 2 == 0 and Z > 1 and D % (2 * S * 16) == 0 and Z % groups == 0
+                       and all(w * groups % (128 * Z) == 0 for w in parts))
         cfg = (S, DP, R, L, D, FF, reduce_here)
         VM = pltpu.VMEM
         DMA = pltpu.SemaphoreType.DMA
         scratch = dict(
-            wT=VM((3, D, D), BF), bcol=VM((2, D, 128), F32), stream=VM((R, L, D), F32), gstream=VM((R, L, D), F32),
-            gmid=VM((R, L, D), F32), nall=VM((2, R, S * L, D), BF), xh1=VM((2, R, L, D), F32), rs1=VM((2, R, L, 128), F32),
+            wT=VM((3 * D, D), BF), wupT=VM((FF, D), BF), wdnT=VM((D, FF), BF), bcol=VM((2, D, 128), F32),
+            stream=VM((R, L, D), F32), gstream=VM((R, L, D), F32), gmid=VM((R, L, D), F32), nall=VM((2, R, S * L, D), BF), xh1=VM((2, R, L, D), F32), rs1=VM((2, R, L, 128), F32),
             xh2=VM((2, R, L, D), F32), rs2=VM((2, R, L, 128), F32), n2T=VM((2, R, D, L), BF), qT=VM((D, L), BF),
             qn=VM((2, R, L, D), BF), linv=VM((2, R, HEADS, 8, L), F32), oT=VM((2, R, D, L), BF),
             hidden=VM((2, R, L, FF), BF), slope=VM((2, R, L, FF), F32), e_scr=VM((2, R, S * L, HEADS * L), BF),
-            pg_out=VM((2, R, S - 1, L, D), BF), pg_in=VM((2, R, S - 1, L, D), BF), vec=VM((8, W), F32),
-            nsend=DMA((2, R, X + 1)), fsend=DMA((2, R, X)), nrecv=DMA((2, R, S)), psend=DMA((2, R, S)), precv=DMA((2, R, S)),
-            out_sem=DMA)
+            pair_out=VM((2, R, X - 1, L, D), BF), pair_in=VM((2, R, X - 1, L, D), BF), part_out=VM((2, R, X - 1, L, D), BF),
+            part_in=VM((2, R, X - 1, L, D), BF), near_out=VM((2, R, L, D), BF), near_in=VM((2, R, L, D), BF),
+            keep=VM((R, X - 1, L, D), F32), vec=VM((8, W), F32),
+            nsend=DMA((2, R, X + 1)), fsend=DMA((2, R, X)), nrecv=DMA((2, R, S)), psend=DMA((2, 2, R, X)), precv=DMA((2, 2, R, X)),
+            nearsem=DMA((2, 2, R)), out_sems=DMA((3, R)), gw_sem=DMA((2,)), in_sem=DMA((len(LOADS),)))
         if reduce_here:
-            most = max(Z, X) - 1
+            lines = W // 128
             scratch.update(
-                stage=VM((D, W), BF), gath=VM((D, W), BF), vs_seq=VM((S, W // 128, 128), F32), vs_dp=VM((DP, W // 128, 128), F32),
-                vss=DMA((S - 1,)), vsr=DMA((S - 1,)), vds=DMA((DP - 1,)), vdr=DMA((DP - 1,)))
+                stage=VM((D, W), BF), gath=VM((D, W), BF), vs1=VM((2, lines, 128), F32), vs2=VM((S, lines, 128), F32),
+                vs3=VM((Z, lines, 128), F32), vss1=DMA((1,)), vsr1=DMA((1,)), vss2=DMA((S - 1,)), vsr2=DMA((S - 1,)),
+                vss3=DMA((Z - 1,)), vsr3=DMA((Z - 1,)))
+            most = max(S, Z) - 1
             for p, w in enumerate(parts):
                 scratch.update({
-                    f"r1_{p}": VM((D // 2, w), BF), f"r2_{p}": VM((D // 4, w), BF), f"r3_{p}": VM((Z - 1, D // 4 // Z, w), BF),
-                    f"r4_{p}": VM((X - 1, D // 4 // Z, w // X), BF), f"ss_{p}": DMA((8, most)), f"sr_{p}": DMA((8, most))})
+                    f"r1_{p}": VM((D // 2, w), BF), f"r2_{p}": VM((S - 1, h2, w), BF), f"r3_{p}": VM((Z - 1, 16, w * groups // Z), BF),
+                    f"ss_{p}": DMA((6, most)), f"sr_{p}": DMA((6, most))})
         vm = pl.BlockSpec(memory_space=pltpu.VMEM)
         sm = pl.BlockSpec(memory_space=pltpu.SMEM)
         hbm = pl.BlockSpec(memory_space=pl.ANY)
@@ -635,10 +754,11 @@
         outs = dict(
             y=shape((R, L, D), BF), g1=shape((R, L, D), F32), ge=shape((R, L, D), F32),
             gw=shape((D, W), BF if reduce_here else F32), gv=shape((W // 128, 128), F32))
-        names = (*ins, *outs, *scratch)
+        scratch.update({n: VM(ins[n].shape, ins[n].dtype) for n in LOADS})
+        names = (*(n if n == "lengths" else n + "_in" for n in ins), *outs, *scratch)
         y, g1, ge, gw, gv = pl.pallas_call(
             functools.partial(block_kernel, cfg, names), out_shape=tuple(outs.values()),
-            in_specs=[sm if n == "lengths" else vm for n in ins], out_specs=tuple(hbm if n == "gw" else vm for n in outs),
+            in_specs=[sm if n == "lengths" else hbm for n in ins], out_specs=tuple(vm if n == "gv" else hbm for n in outs),
             scratch_shapes=list(scratch.values()),
             compiler_params=pltpu.CompilerParams(collective_id=0, has_side_effects=True, vmem_limit_bytes=VMEM_LIMIT),
         )(*ins.values())

time: 129 us -> 99.6 us (0.77); the launches traced: 126 us -> 99.4 us
  Pallas kernels: 126 us -> 98.6 us
    pallas_call x1, Pallas kernels: 121 us -> 93.9 us  [shards(): pl.pallas_call(functools.partial(block_kernel, cfg, names), out_shape=tup...]
where the time goes in v2:
time: 99.6 us; the launch traced here: 99.4 us
  Pallas kernels  98.6 us (99%)
    pallas_call x1, Pallas kernels, shards(): pl.pallas_call(functools.partial(block_kernel, cfg, names), out_shape=tup...  93.9 us
    pallas_call x1, Pallas kernels, shards(): pl.pallas_call(functools.partial(finish_kernel, D, FF, (*outs, *ends, *te...  4.66 us

profile of v2, /device:TPU:0, one launch (start us, length us, event | category | flops | bytes accessed | tf_op | source)
XLA Modules:
  0.0 99.4 jit_solution(4632034902489962686)
XLA Ops:
  0.7 93.9 %shard_map.271 = (bf16[3,256,256]{2,1,0:T(8,128)(2,1)}, f32[3,256,256]{2,1,0:T(8,128)}, f32[3,256,256]{2,1,0:T(8,128)}, bf16[256,3072]{1,0:T(8,128)(2,1)}, f32[24,128]{1,0:T(8,128)}) custom-call(bf16[3,256,256]{2,1,0:T(8,128)(2,1)} %bitcast.20, bf16[3,256,256]{2,1,0:T(8,128)(2,1)} %bitcast.21, bf16[3,256,256]{2,1,0:T(8,128)(2,1)} %bitcast.22, s32[3]{0:T(128)} %refs_3_.1, ...), custom_call_target="tpu_custom_call" | custom-call | tf_op jit(solution)/shard_map/pallas_call | solution.py:759
  94.6 4.7 %shard_map.272 = (bf16[3,256,256]{2,1,0:T(8,128)(2,1)}, f32[3,256,256]{2,1,0:T(8,128)}, f32[3,256,256]{2,1,0:T(8,128)}, f32[1,256]{1,0:T(1,128)}, f32[1,256]{1,0...) custom-call(bf16[3,256,256]{2,1,0:T(8,128)(2,1)} %get-tuple-element., ...), custom_call_target="tpu_custom_call" | custom-call | tf_op jit(solution)/shard_map/pallas_call | solution.py:776

commit v3 on v2

--- a/solution.py
+++ b/solution.py
@@ -15,7 +15,7 @@
 BF = jnp.bfloat16
 F32 = jnp.float32
 MESH = pl.DeviceIdType.MESH
-VMEM_LIMIT = 60 * 1024 * 1024
+VMEM_LIMIT = 61 * 1024 * 1024
 
 
 def nn(a, b):
@@ -46,10 +46,10 @@
 
 def gelu_parts(x):
     c0 = 0.7978845608028654
+    c1 = c0 * 0.044715
     x2 = x * x
-    t = jnp.tanh(c0 * (x + 0.044715 * (x2 * x)))
-    half = 0.5 * (1.0 + t)
-    slope = half + (0.5 * x) * (1.0 - t * t) * (c0 * (1.0 + (3 * 0.044715) * x2))
+    half = 0.5 + 0.5 * jnp.tanh(x * (c0 + c1 * x2))
+    slope = half + (half * (1.0 - half)) * (x * (2 * c0 + (6 * c1) * x2))
     return x * half, slope
 
 
@@ -74,62 +74,62 @@
 
 
 class Share:
-    def __init__(self, v, start, w, into):
-        self.v, self.start_lane = v, start
-        self.cols = slice(start, start + w)
-        self.r1, self.r2, self.r3, self.send, self.recv = into
-        self.n2, self.n3 = v.S, v.DP // 2
-        self.h1 = v.D // 2
-        self.h2 = self.h1 // self.n2
-        self.groups = self.h2 // 16
-        self.w3 = w * self.groups // self.n3
-        self.b1 = v.core * self.h1
-        self.b2 = self.b1 + v.spot2 * self.h2
-
-    def rows(self, base, n):
-        return pl.ds(pl.multiple_of(base, 16), n)
-
-    def chunk(self, z):
-        row, lane = lax.rem(z, self.groups), lax.div(z, self.groups)
-        return self.rows(self.b2 + row * 16, 16), pl.ds(pl.multiple_of(self.start_lane + lane * self.w3, 128), self.w3)
+    def __init__(self, v, start, w, into, stages, whole_last):
+        self.v, self.stages, self.whole = v, stages, whole_last
+        self.bufs, self.send, self.recv = into
+        self.down = len(stages)
+        self.steps = 2 * self.down - (1 if whole_last else 0)
+        self.plan = share_plan(v.D, w, [n for n, _, _ in stages], whole_last)
+        base = (0, start)
+        self.bases = [base]
+        for k, (n, own, _) in enumerate(stages):
+            base = self.part(k, own)[0]
+            self.bases.append(base)
+
+    def part(self, k, number):
+        rows, lanes, row_parts, _ = self.plan[k]
+        r, c = self.bases[k]
+        if row_parts == 1:
+            return (r, c + number * lanes), (rows, lanes)
+        return (r + lax.rem(number, row_parts) * rows, c + lax.div(number, row_parts) * lanes), (rows, lanes)
+
+    def window(self, base, size):
+        r, c = base
+        at = c if isinstance(c, int) else pl.multiple_of(c, 128)
+        return pl.ds(pl.multiple_of(r, 16) if not isinstance(r, int) else r, size[0]), pl.ds(at, size[1])
+
+    def region(self, k):
+        rows, lanes, row_parts, lane_parts = self.plan[k]
+        return self.window(self.bases[k], (rows * row_parts, lanes * lane_parts))
 
     def copies(self, i):
         v = self.v
-        if i == 1:
-            return [(v.stage.at[self.rows((1 - v.core) * self.h1, self.h1), self.cols], self.r1, v.sibling)]
-        if i == 6:
-            ref = v.gath.at[self.rows(self.b1, self.h1), self.cols]
-            return [(ref, ref, v.sibling)]
+        k = i if i < self.down else 2 * self.down - 1 - i - (1 if self.whole else 0)
+        n, own, device = self.stages[k]
         out = []
-        if i in (2, 5):
-            for j in range(1, self.n2):
-                other = lax.rem(v.spot2 + j, self.n2)
-                if i == 2:
-                    src = v.stage.at[self.rows(self.b1 + other * self.h2, self.h2), self.cols]
-                    out.append((src, self.r2.at[j - 1], v.in_plane(other)))
-                else:
-                    ref = v.gath.at[self.rows(self.b2, self.h2), self.cols]
-                    out.append((ref, ref, v.in_plane(other)))
-            return out
-        for j in range(1, self.n3):
-            other = lax.rem(v.spot3 + j, self.n3)
-            if i == 3:
-                out.append((v.stage.at[self.chunk(other)], self.r3.at[j - 1], v.across(other)))
+        for j in range(1, n):
+            other = lax.rem(own + j, n)
+            if i == self.down - 1 and self.whole:
+                out.append((v.stage.at[self.region(k)], self.bufs[k].at[own], device(other)))
+            elif i < self.down:
+                out.append((v.stage.at[self.window(*self.part(k, other))], self.bufs[k].at[j - 1], device(other)))
             else:
-                ref = v.gath.at[self.chunk(v.spot3)]
-                out.append((ref, ref, v.across(other)))
+                ref = v.gath.at[self.window(*self.part(k, own))]
+                out.append((ref, ref, device(other)))
         return out
 
     def made(self, i):
-        return [pltpu.make_async_remote_copy(src_ref=s, dst_ref=d, send_sem=self.send.at[i - 1, j], recv_sem=self.recv.at[i - 1, j],
+        return [pltpu.make_async_remote_copy(src_ref=s, dst_ref=d, send_sem=self.send.at[i, j], recv_sem=self.recv.at[i, j],
                                              device_id=dev, device_id_type=MESH)
                 for j, (s, d, dev) in enumerate(self.copies(i))]
 
     def start(self, i):
         v = self.v
-        if i == 1:
-            there = self.rows((1 - v.core) * self.h1, self.h1)
-            v.stage[there, self.cols] = v.dW[there, self.cols].astype(BF)
+        if i == 0:
+            n, own, _ = self.stages[0]
+            for j in range(1, n):
+                there = self.window(*self.part(0, lax.rem(own + j, n)))
+                v.stage[there] = v.dW[there].astype(BF)
         for c in self.made(i):
             c.start()
 
@@ -137,18 +137,21 @@
         v = self.v
         for c in self.made(i):
             c.wait()
-        if i > 3:
+        if i >= self.down:
             return
-        if i == 1:
-            at, got = (self.rows(self.b1, self.h1), self.cols), [self.r1]
-        elif i == 2:
-            at, got = (self.rows(self.b2, self.h2), self.cols), [self.r2.at[j] for j in range(self.n2 - 1)]
+        n, own, _ = self.stages[i]
+        if i == self.down - 1 and self.whole:
+            at = self.region(i)
+            self.bufs[i][own] = v.stage[at]
+            total = self.bufs[i][0].astype(F32)
+            for j in range(1, n):
+                total = total + self.bufs[i][j].astype(F32)
         else:
-            at, got = self.chunk(v.spot3), [self.r3.at[j] for j in range(self.n3 - 1)]
-        total = v.dW[at]
-        for g in got:
-            total = total + g[...].astype(F32)
-        if i == 3:
+            at = self.window(*self.part(i, own))
+            total = v.dW[at]
+            for j in range(n - 1):
+                total = total + self.bufs[i][j].astype(F32)
+        if i == self.down - 1:
             v.gath[at] = total.astype(BF)
         else:
             v.dW[at] = total
@@ -156,8 +159,31 @@
 
     def step(self, i):
         self.finish(i)
-        if i < 6:
+        if i + 1 < self.steps:
             self.start(i + 1)
+
+
+def share_plan(D, w, members, whole_last):
+    rows, lanes, plan = D, w, []
+    for k, n in enumerate(members):
+        if whole_last and k == len(members) - 1:
+            plan.append((rows, lanes, 1, 1))
+            continue
+        row_parts = max(p for p in range(1, n + 1) if n % p == 0 and rows % (16 * p) == 0)
+        lane_parts = n // row_parts
+        if lanes % (128 * lane_parts):
+            return None
+        rows, lanes = rows // row_parts, lanes // lane_parts
+        plan.append((rows, lanes, row_parts, lane_parts))
+    return plan
+
+
+def part_shapes(D, w, members, whole_last):
+    shapes = []
+    for k, (n, (rows, lanes, rp, lp)) in enumerate(zip(members, share_plan(D, w, members, whole_last))):
+        whole = whole_last and k == len(members) - 1
+        shapes.append((n if whole else n - 1, rows, lanes))
+    return shapes
 
 
 class SmallSum:
@@ -325,7 +351,6 @@
         length = v.lengths[r]
         rows = v.nall[a, r, 0:KB, :]
         keys = nn(rows, v.wqkv[:, D:2 * D]).astype(BF)
-        VT = (nt(v.wT[2 * D:], rows) + wide(v.bcol[1], KB)).astype(BF)
         qT = v.qT[...]
         for t in range(nb):
             key_pos = t * L + lax.broadcasted_iota(jnp.int32, (L, L), 0)
@@ -336,14 +361,20 @@
             s = nn(keys[:, pair(h)], head_rows(qT, h)) + bias[0:KB]
             s_scr[0:KB, h * L:(h + 1) * L] = s
             tops.append(jnp.max(jnp.max(s.reshape(KB // 8, 8, L), axis=0), axis=0, keepdims=True))
+        VT = (nt(v.wT[2 * D:], rows) + wide(v.bcol[1], KB)).astype(BF)
         for h in range(HEADS):
-            hs = slice(h * HD, (h + 1) * HD)
-            e = jnp.exp(s_scr[0:KB, h * L:(h + 1) * L] - tops[h])
-            inv = 1.0 / jnp.sum(fold(e), axis=0, keepdims=True)
-            low = e.astype(BF)
-            v.e_scr[a, r, 0:KB, h * L:(h + 1) * L] = low
+            hs, hl = slice(h * HD, (h + 1) * HD), slice(h * L, (h + 1) * L)
+            sums, out = [], []
+            for t in range(nb):
+                ts = slice(t * L, (t + 1) * L)
+                e = jnp.exp(s_scr[ts, hl] - tops[h])
+                sums.append(fold(e))
+                low = e.astype(BF)
+                v.e_scr[a, r, ts, hl] = low
+                out.append(nn(VT[hs, ts], low))
+            inv = 1.0 / jnp.sum(sum(sums), axis=0, keepdims=True)
             v.linv[a, r, h] = jnp.broadcast_to(inv, (8, L))
-            v.oT[a, r, hs] = (nn(VT[hs], low) * inv).astype(BF)
+            v.oT[a, r, hs] = (sum(out) * inv).astype(BF)
 
     def forward_all(bias, s_scr):
         hand_on(0, 0)
@@ -388,7 +419,8 @@
     VM = pltpu.VMEM
     pl.run_scoped(forward_all, VM((S * L, L), F32), VM((S * L, HEADS * L), F32))
     pl.run_scoped(functools.partial(backward, v, with_size), VM((R, D, L), BF), VM((R, L, FF), BF), VM((R, L, D), BF),
-                  VM((R, L, 3 * D), BF), VM((D, W), F32), VM((L, D), F32))
+                  VM((R, L, 3 * D), BF), VM((D, W), F32), VM((L, D), F32),
+                  VM((S * L, D), BF), VM((S * L, 2 * D), BF))
 
     for a in range(2):
         for r in range(R):
@@ -399,7 +431,7 @@
                 handed_on(a, r, c).wait_send()
 
 
-def backward(v, with_size, gbT, gpre, ga_s, gqkv, dW, gns):
+def backward(v, with_size, gbT, gpre, ga_s, gqkv, dW, gns, pg_s, gkv_s):
     S, DP, R, L, D, FF, W = v.S, v.DP, v.R, v.L, v.D, v.FF, v.W
     me, dp, mine = v.me, v.dp, v.mine
     v.dW = dW
@@ -411,25 +443,36 @@
 
     def pair_copy(a, r, c):
         return pltpu.make_async_remote_copy(
-            src_ref=v.pair_out.at[a, r, c], dst_ref=v.pair_in.at[a, r, c], send_sem=v.psend.at[0, a, r, c],
+            src_ref=v.pair_out.at[r, c], dst_ref=v.pair_in.at[a, r, c], send_sem=v.psend.at[0, a, r, c],
             recv_sem=v.precv.at[0, a, r, c], device_id=v.sibling, device_id_type=MESH)
 
     def part_copy(a, r, src, dst):
         return pltpu.make_async_remote_copy(
-            src_ref=v.part_out.at[a, r, dst], dst_ref=v.part_in.at[a, r, src - 1], send_sem=v.psend.at[1, a, r, dst],
+            src_ref=v.part_out.at[r, dst], dst_ref=v.part_in.at[a, r, src - 1], send_sem=v.psend.at[1, a, r, dst],
             recv_sem=v.precv.at[1, a, r, src], device_id=(dp, 2 * dst + core), device_id_type=MESH)
 
     def near_copy(a, r):
         return pltpu.make_async_remote_copy(
-            src_ref=v.near_out.at[a, r], dst_ref=v.near_in.at[a, r], send_sem=v.nearsem.at[0, a, r],
+            src_ref=v.near_out.at[r], dst_ref=v.near_in.at[a, r], send_sem=v.nearsem.at[0, a, r],
             recv_sem=v.nearsem.at[1, a, r], device_id=v.sibling, device_id_type=MESH)
 
     def pass_on(a, r):
         @pl.loop(0, chip)
         def _(c):
             pair_copy(a, r, c).wait_recv()
-            v.part_out[a, r, c] = (v.keep[r, c] + v.pair_in[a, r, c].astype(F32)).astype(BF)
+            v.part_out[r, c] = (v.keep[r, c].astype(F32) + v.pair_in[a, r, c].astype(F32)).astype(BF)
             part_copy(a, r, chip, c).start()
+
+    def sent(a):
+        for r in range(R):
+            @pl.loop(0, chip)
+            def _(c):
+                pair_copy(a, r, c).wait_send()
+                part_copy(a, r, chip, c).wait_send()
+
+            @pl.when(core == 1)
+            def _():
+                near_copy(a, r).wait_send()
 
     def add_vec(start, terms):
         v.vec[:, start:start + terms.shape[1]] += fold(terms)
@@ -466,40 +509,44 @@
         rows = v.nall[a, r, 0:KB, :]
         values = (nn(rows, v.wqkv[:, 2 * D:]) + v.qvb[1:2, :]).astype(BF)
         KT = nt(v.wT[D:2 * D], rows).astype(BF)
-        gv = nn(v.e_scr[a, r, 0:KB, :], heads_apart(gaT_n.T))
+        blocks = [slice(t * L, (t + 1) * L) for t in range(nb)]
+        ga_apart, q_apart = heads_apart(gaT_n.T), heads_apart(v.qn[a, r])
+        for ts in blocks:
+            gkv_s[ts, D:] = nn(v.e_scr[a, r, ts, :], ga_apart).astype(BF)
         for h in range(HEADS):
             hl = slice(h * L, (h + 1) * L)
             gp = nn(values[:, pair(h)], head_rows(gaT_n, h))
             v.e_scr[a, r, 0:KB, hl] = (v.e_scr[a, r, 0:KB, hl].astype(F32) * (gp - deltas[h])).astype(BF)
         tick()
-        gk = nn(v.e_scr[a, r, 0:KB, :], heads_apart(v.qn[a, r]))
-        gkv = jnp.concatenate([gk, gv], axis=1).astype(BF)
-        gqT = jnp.concatenate([nn(KT[h * HD:(h + 1) * HD], v.e_scr[a, r, 0:KB, h * L:(h + 1) * L]) for h in range(HEADS)], axis=0)
-        pg = nn(gkv, v.wT[D:])
+        for ts in blocks:
+            gkv_s[ts, :D] = nn(v.e_scr[a, r, ts, :], q_apart).astype(BF)
+        for ts in blocks:
+            pg_s[ts] = nn(gkv_s[ts, :], v.wT[D:]).astype(BF)
         for t in range(nb):
-            block = pg[t * L:(t + 1) * L]
+            ts = blocks[t]
             if t // 2 < nb // 2 - 1:
                 @pl.when((t // 2 < chip) & (t % 2 == core))
                 def _():
-                    v.keep[r, t // 2] = block
+                    v.keep[r, t // 2] = pg_s[ts]
 
                 @pl.when((t // 2 < chip) & (t % 2 != core))
                 def _():
-                    v.pair_out[a, r, t // 2] = block.astype(BF)
+                    v.pair_out[r, t // 2] = pg_s[ts]
                     pair_copy(a, r, t // 2).start()
 
             if t % 2 == 0:
                 @pl.when(t == me - 1)
                 def _():
-                    v.near_out[a, r] = block.astype(BF)
+                    v.near_out[r] = pg_s[ts]
                     near_copy(a, r).start()
 
             @pl.when(t == me)
             def _():
-                gqkv[r, :, D:] = gkv[t * L:(t + 1) * L]
-
-        add_vec(V_VB, gkv[:, D:].astype(F32))
-        dW[:, QW + D:QW + 3 * D] += nn(rows.T, gkv)
+                gqkv[r, :, D:] = gkv_s[ts]
+
+        add_vec(V_VB, gkv_s[0:KB, D:].astype(F32))
+        gqT = jnp.concatenate([nn(KT[h * HD:(h + 1) * HD], v.e_scr[a, r, 0:KB, h * L:(h + 1) * L]) for h in range(HEADS)], axis=0)
+        dW[:, QW + D:QW + 3 * D] += nn(rows.T, gkv_s[0:KB])
         gq = (gqT * (HD ** -0.5)).T.astype(BF)
         gqkv[r, :, :D] = gq
         add_vec(V_QB, gq.astype(F32))
@@ -544,8 +591,11 @@
     dW[:, QW + D:QW + 3 * D] = jnp.zeros((D, 2 * D), F32)
     reducing = v.reduce_here
     if reducing:
-        into = lambda p: tuple(getattr(v, f"{n}_{p}") for n in ("r1", "r2", "r3", "ss", "sr"))
-        up, down, qkv = (Share(v, start, w, into(p)) for p, (start, w) in enumerate(((UP, FF), (DN, FF + D), (QW, 3 * D))))
+        pair_stage = (2, core, lambda n: v.sibling)
+        plane, across = (S, v.spot2, v.in_plane), (DP // 2, v.spot3, v.across)
+        into = lambda p: ([getattr(v, f"b{k}_{p}") for k in range(3)], getattr(v, f"ss_{p}"), getattr(v, f"sr_{p}"))
+        up, down, qkv = (Share(v, start, w, into(p), (pair_stage, plane, across), whole)
+                         for p, (start, w, whole) in enumerate(((UP, FF, False), (DN, FF + D, False), (QW, 3 * D, True))))
         small = SmallSum(v)
 
     def nothing():
@@ -554,8 +604,7 @@
     def attention(a, r, tick):
         with_size(functools.partial(attention_core, a, r, tick if reducing else nothing))
 
-    @pl.loop(0, R)
-    def _(r):
+    for r in range(R):
         backward_mlp(1, r)
 
     weight_terms(1, every, ("up", "down"))
@@ -576,34 +625,37 @@
         v.stream[r] = v.gstream[r]
         backward_mlp(0, r)
 
-    pl.loop(0, R - 1)(between)
+    for r in range(R - 1):
+        between(r)
     if early:
         weight_terms(0, early, ("up", "down"))
     between(R - 1)
     weight_terms(0, last, ("up",))
     if reducing:
-        up.start(1)
+        up.start(0)
     weight_terms(0, last, ("down",))
     if reducing:
-        down.start(1)
+        down.start(0)
+
+    sent(1)
 
     def tick_first():
+        up.step(0)
+        down.step(0)
+
+    def tick_last():
         up.step(1)
-        down.step(1)
-
-    def tick_last():
-        up.step(2)
 
     for r in range(R):
         attention(0, r, tick_first if r == 0 else tick_last if r == R - 1 else nothing)
         if r > 0:
             pass_on(0, r - 1)
-    if reducing:
-        down.step(2)
     query_terms(0)
     if reducing:
-        qkv.start(1)
+        qkv.start(0)
     pass_on(0, R - 1)
+    if reducing:
+        down.step(1)
 
     def final(r):
         backward_norm(0, r)
@@ -616,29 +668,29 @@
         return jnp.concatenate([sums[:, k * 128:(k + 1) * 128] for k in range(W // 128)], axis=0)
 
     if reducing:
+        gath_copy = lambda k, cols: pltpu.make_async_copy(v.gath.at[:, cols], v.gw.at[:, cols], v.gw_sem.at[k])
+        first_out, second_out = gath_copy(0, slice(0, QW)), gath_copy(1, slice(QW, W))
+        qkv.step(0)
+        for r in range(R - 1):
+            final(r)
+        up.step(2)
         qkv.step(1)
-        pl.loop(0, R - 1)(final)
-        up.step(3)
-        down.step(3)
+        down.step(2)
         final(R - 1)
         small.start(0, small_lines())
+        up.step(3)
+        small.start(1, small.finish(0))
         qkv.step(2)
+        down.step(3)
+        small.start(2, small.finish(1))
         up.step(4)
-        small.start(1, small.finish(0))
+        qkv.step(3)
         down.step(4)
-        qkv.step(3)
-        small.start(2, small.finish(1))
-        up.step(5)
-        down.step(5)
         v.gv[...] = small.finish(2)
-        qkv.step(4)
-        up.finish(6)
-        down.finish(6)
-        gath_copy = lambda k, cols: pltpu.make_async_copy(v.gath.at[:, cols], v.gw.at[:, cols], v.gw_sem.at[k])
-        first_out, second_out = gath_copy(0, slice(0, QW)), gath_copy(1, slice(QW, W))
+        up.finish(5)
+        down.finish(5)
         first_out.start()
-        qkv.step(5)
-        qkv.finish(6)
+        qkv.finish(4)
         second_out.start()
         first_out.wait()
         second_out.wait()
@@ -653,22 +705,16 @@
         out_copy(v, 0, v.hid, v.y, r).wait()
         out_copy(v, 1, v.gstream, v.g1, r).wait()
         out_copy(v, 2, v.gmid, v.ge, r).wait()
-        for a in range(2):
-            @pl.loop(0, chip)
-            def _(c):
-                pair_copy(a, r, c).wait_send()
-                part_copy(a, r, chip, c).wait_send()
-
-            @pl.when(core == 1)
-            def _():
-                near_copy(a, r).wait_send()
+    sent(0)
 
 
 def finish_kernel(D, FF, names, *refs):
     v = types.SimpleNamespace(**dict(zip(names, refs, strict=True)))
     load = lambda i, src, dst: pltpu.make_async_copy(src, dst, v.sems.at[0, i])
     save = lambda i, src, dst: pltpu.make_async_copy(src, dst, v.sems.at[1, i])
-    loads = [load(0, v.gw, v.gw_s), load(1, v.gv, v.gv_s), load(2, v.g1, v.g1_s), load(3, v.ge, v.ge_s), load(4, v.y, v.y_s)]
+    cols = (slice(FF, 2 * FF), slice(0, FF), slice(2 * FF + D, 2 * FF + 4 * D), slice(2 * FF, 2 * FF + D))
+    loads = [load(i, v.gw.at[:, c], v.gw_s.at[:, c]) for i, c in enumerate(cols)]
+    loads += [load(4, v.g1, v.g1_s), load(5, v.ge, v.ge_s), load(6, v.y, v.y_s), load(7, v.gv, v.gv_s)]
     for c in loads:
         c.start()
     saves = []
@@ -677,19 +723,15 @@
         saves.append(save(len(saves), src, dst))
         saves[-1].start()
 
-    loads[0].wait()
-    v.wup_s[...] = v.gw_s[:, 0:FF].astype(F32)
-    keep(v.wup_s, v.wup)
-    v.wdn_s[...] = v.gw_s[:, FF:2 * FF].T.astype(F32)
-    keep(v.wdn_s, v.wdn)
-    v.wqkv_s[...] = v.gw_s[:, 2 * FF + D:].astype(F32)
-    keep(v.wqkv_s, v.wqkv)
-    v.wout_s[...] = v.gw_s[:, 2 * FF:2 * FF + D].astype(F32)
-    keep(v.wout_s, v.wout)
-    for c, src, dst in zip(loads[2:], (v.g1_s, v.ge_s, v.y_s), (v.g1_o, v.ge_o, v.y_o)):
+    for i, (c, src, dst) in enumerate(zip(cols, (v.wdn_s, v.wup_s, v.wqkv_s, v.wout_s), (v.wdn, v.wup, v.wqkv, v.wout))):
+        loads[i].wait()
+        part = v.gw_s[:, c]
+        src[...] = (part.T if i == 0 else part).astype(F32)
+        keep(src, dst)
+    for c, src, dst in zip(loads[4:7], (v.g1_s, v.ge_s, v.y_s), (v.g1_o, v.ge_o, v.y_o)):
         c.wait()
         keep(src, dst)
-    loads[1].wait()
+    loads[7].wait()
     n = D // 128
     at = 0
     for ref, size in ((v.ln1g, n), (v.ln1b, n), (v.qvb, 2 * n), (v.bout, n), (v.ln2g, n), (v.ln2b, n), (v.bdn, n),
@@ -712,10 +754,8 @@
         W = 4 * D + 2 * FF
         X, Z = S // 2, DP // 2
         parts = (FF, FF + D, 3 * D)
-        h2 = D // 2 // S
-        groups = max(h2 // 16, 1)
-        reduce_here = (DP % 2 == 0 and Z > 1 and D % (2 * S * 16) == 0 and Z % groups == 0
-                       and all(w * groups % (128 * Z) == 0 for w in parts))
+        members, wholes = (2, S, Z), (False, False, True)
+        reduce_here = DP % 2 == 0 and Z > 1 and all(share_plan(D, w, members, f) for w, f in zip(parts, wholes))
         cfg = (S, DP, R, L, D, FF, reduce_here)
         VM = pltpu.VMEM
         DMA = pltpu.SemaphoreType.DMA
@@ -725,9 +765,9 @@
             xh2=VM((2, R, L, D), F32), rs2=VM((2, R, L, 128), F32), n2T=VM((2, R, D, L), BF), qT=VM((D, L), BF),
             qn=VM((2, R, L, D), BF), linv=VM((2, R, HEADS, 8, L), F32), oT=VM((2, R, D, L), BF),
             hidden=VM((2, R, L, FF), BF), slope=VM((2, R, L, FF), F32), e_scr=VM((2, R, S * L, HEADS * L), BF),
-            pair_out=VM((2, R, X - 1, L, D), BF), pair_in=VM((2, R, X - 1, L, D), BF), part_out=VM((2, R, X - 1, L, D), BF),
-            part_in=VM((2, R, X - 1, L, D), BF), near_out=VM((2, R, L, D), BF), near_in=VM((2, R, L, D), BF),
-            keep=VM((R, X - 1, L, D), F32), vec=VM((8, W), F32),
+            pair_out=VM((R, X - 1, L, D), BF), pair_in=VM((2, R, X - 1, L, D), BF), part_out=VM((R, X - 1, L, D), BF),
+            part_in=VM((2, R, X - 1, L, D), BF), near_out=VM((R, L, D), BF), near_in=VM((2, R, L, D), BF),
+            keep=VM((R, X - 1, L, D), BF), vec=VM((8, W), F32),
             nsend=DMA((2, R, X + 1)), fsend=DMA((2, R, X)), nrecv=DMA((2, R, S)), psend=DMA((2, 2, R, X)), precv=DMA((2, 2, R, X)),
             nearsem=DMA((2, 2, R)), out_sems=DMA((3, R)), gw_sem=DMA((2,)), in_sem=DMA((len(LOADS),)))
         if reduce_here:
@@ -737,10 +777,10 @@
                 vs3=VM((Z, lines, 128), F32), vss1=DMA((1,)), vsr1=DMA((1,)), vss2=DMA((S - 1,)), vsr2=DMA((S - 1,)),
                 vss3=DMA((Z - 1,)), vsr3=DMA((Z - 1,)))
             most = max(S, Z) - 1
-            for p, w in enumerate(parts):
-                scratch.update({
-                    f"r1_{p}": VM((D // 2, w), BF), f"r2_{p}": VM((S - 1, h2, w), BF), f"r3_{p}": VM((Z - 1, 16, w * groups // Z), BF),
-                    f"ss_{p}": DMA((6, most)), f"sr_{p}": DMA((6, most))})
+            for p, (w, f) in enumerate(zip(parts, wholes)):
+                for k, dims in enumerate(part_shapes(D, w, members, f)):
+                    scratch[f"b{k}_{p}"] = VM(dims, BF)
+                scratch.update({f"ss_{p}": DMA((6, most)), f"sr_{p}": DMA((6, most))})
         vm = pl.BlockSpec(memory_space=pltpu.VMEM)
         sm = pl.BlockSpec(memory_space=pltpu.SMEM)
         hbm = pl.BlockSpec(memory_space=pl.ANY)
@@ -772,7 +812,7 @@
         temps = dict(
             y_s=VM((R, L, D), BF), g1_s=VM((R, L, D), F32), ge_s=VM((R, L, D), F32), gw_s=VM((D, W), gw.dtype),
             gv_s=VM((W // 128, 128), F32), wup_s=VM((D, FF), F32), wdn_s=VM((FF, D), F32), wqkv_s=VM((D, 3 * D), F32),
-            wout_s=VM((D, D), F32), sems=DMA((2, 7)))
+            wout_s=VM((D, D), F32), sems=DMA((2, 8)))
         res = pl.pallas_call(
             functools.partial(finish_kernel, D, FF, (*outs, *ends, *temps)), out_shape=full, in_specs=[hbm] * 5,
             out_specs=[hbm if n in large else vm for n in ends], scratch_shapes=list(temps.values()),

time: 99.6 us -> 92.9 us (0.933)
  Pallas kernels: 98.6 us -> 91.9 us
    pallas_call x1, Pallas kernels: 93.9 us -> 87.6 us  [shards(): pl.pallas_call(functools.partial(block_kernel, cfg, names), out_shape=tup...]
where the time goes in v3:
time: 92.9 us; the launch traced here: 92.8 us
  Pallas kernels  91.9 us (99%)
    pallas_call x1, Pallas kernels, shards(): pl.pallas_call(functools.partial(block_kernel, cfg, names), out_shape=tup...  87.6 us
    pallas_call x1, Pallas kernels, shards(): pl.pallas_call(functools.partial(finish_kernel, D, FF, (*outs, *ends, *te...  4.3 us

profile of v3, /device:TPU:0, one launch (start us, length us, event | category | flops | bytes accessed | tf_op | source)
XLA Modules:
  0.0 92.8 jit_solution(15952336209093230467)
XLA Ops:
  0.7 87.6 %shard_map.271 = (bf16[3,256,256]{2,1,0:T(8,128)(2,1)}, f32[3,256,256]{2,1,0:T(8,128)}, f32[3,256,256]{2,1,0:T(8,128)}, bf16[256,3072]{1,0:T(8,128)(2,1)}, f32[24,128]{1,0:T(8,128)}) custom-call(bf16[3,256,256]{2,1,0:T(8,128)(2,1)} %bitcast.20, bf16[3,256,256]{2,1,0:T(8,128)(2,1)} %bitcast.21, bf16[3,256,256]{2,1,0:T(8,128)(2,1)} %bitcast.22, s32[3]{0:T(128)} %refs_3_.1, ...), custom_call_target="tpu_custom_call" | custom-call | tf_op jit(solution)/shard_map/pallas_call | solution.py:799
  88.3 4.3 %shard_map.272 = (bf16[3,256,256]{2,1,0:T(8,128)(2,1)}, f32[3,256,256]{2,1,0:T(8,128)}, f32[3,256,256]{2,1,0:T(8,128)}, f32[1,256]{1,0:T(1,128)}, f32[1,256]{1,0...) custom-call(bf16[3,256,256]{2,1,0:T(8,128)(2,1)} %get-tuple-element., ...), custom_call_target="tpu_custom_call" | custom-call | tf_op jit(solution)/shard_map/pallas_call | solution.py:816

commit v4 on v3

--- a/solution.py
+++ b/solution.py
@@ -240,15 +240,44 @@
             low = n
 
     barrier = pltpu.get_barrier_semaphore()
-    peers = [v.sibling] + [(dp, lax.rem(me + 2 * k, S)) for k in range(1, X)]
+    Z = DP // 2
+    x_peers = [(dp, lax.rem(me + 2 * k, S)) for k in range(1, X)]
+    peers, count = [v.sibling] + x_peers, X
     if reduce_here:
         v.spot2, v.spot3 = chip * 2 + lax.rem(dp, 2), lax.div(dp, 2)
         v.in_plane = lambda n: (lax.div(dp, 2) * 2 + lax.rem(n, 2), lax.div(n, 2) * 2 + core)
         v.across = lambda n: (n * 2 + lax.rem(dp, 2), me)
-        peers += [(dp + 1 - 2 * lax.rem(dp, 2), lax.rem(me + 2 * k, S)) for k in range(X)]
-        peers += [v.across(lax.rem(v.spot3 + k, DP // 2)) for k in range(1, DP // 2)]
+        z = v.spot3
+        peers.append((dp + 1 - 2 * lax.rem(dp, 2), me))
+        count = count + 1 + jnp.where(z > 0, 1, 0) + jnp.where(z < Z - 1, 1, 0)
     for peer in peers:
         pl.semaphore_signal(barrier, inc=1, device_id=peer, device_id_type=MESH)
+    if reduce_here:
+        for there, step in ((z < Z - 1, 1), (z > 0, -1)):
+            @pl.when(there)
+            def _():
+                pl.semaphore_signal(barrier, inc=1, device_id=v.across(z + step), device_id_type=MESH)
+
+    def tell(which, peer):
+        pl.semaphore_signal(v.relay.at[which], inc=1, device_id=peer, device_id_type=MESH)
+
+    def first_word():
+        for peer in x_peers:
+            tell(0, peer)
+
+        @pl.when((z > 0) & (z < Z - 1))
+        def _():
+            tell(1, v.across(z + 1))
+            tell(2, v.across(z - 1))
+
+    def passed_on():
+        pl.semaphore_wait(v.relay.at[0], X - 1)
+        pl.when(z >= 2)(lambda: pl.semaphore_wait(v.relay.at[1], 1))
+        pl.when(z <= Z - 3)(lambda: pl.semaphore_wait(v.relay.at[2], 1))
+        pl.when((z >= 2) & (z < Z - 1))(lambda: tell(3, v.across(z + 1)))
+        pl.when((z <= Z - 3) & (z > 0))(lambda: tell(4, v.across(z - 1)))
+        pl.when(z >= 3)(lambda: pl.semaphore_wait(v.relay.at[3], 1))
+        pl.when(z <= Z - 4)(lambda: pl.semaphore_wait(v.relay.at[4], 1))
 
     brought = {}
     for k, name in enumerate(LOADS):
@@ -313,6 +342,14 @@
         def _():
             normed_copy(a, r, me - 1, v.nsend.at[a, r, X], me).wait_recv()
 
+    need("hid", "emb", "ln1g", "ln1b")
+    ln1g, ln1b = v.ln1g[...], v.ln1b[...]
+
+    def first_input(r):
+        v.stream[r] = v.hid[r].astype(F32)
+        first_norm(0, r)
+
+    first_input(0)
     @pl.loop(me + 1, S)
     def _(t):
         for a in range(2):
@@ -320,14 +357,16 @@
                 v.nall[a, r, pl.ds(pl.multiple_of(t * L, L), L)] = jnp.zeros((L, D), BF)
 
     v.vec[...] = jnp.zeros_like(v.vec)
-    need("hid", "emb", "ln1g", "ln1b")
-    ln1g, ln1b = v.ln1g[...], v.ln1b[...]
-
-    @pl.loop(0, R)
+    pl.semaphore_wait(barrier, count)
+    announce(0, 0)
+
+    @pl.loop(1, R)
     def _(r):
-        v.stream[r] = v.hid[r].astype(F32)
-        first_norm(0, r)
-
+        first_input(r)
+        announce(0, r)
+
+    if reduce_here:
+        first_word()
     need("wqkv", "qvb")
     for k in range(3):
         v.wT[k * D:(k + 1) * D] = v.wqkv[:, k * D:(k + 1) * D].T
@@ -339,26 +378,17 @@
         v.wupT[ks] = v.wup[:, ks].T
         v.wdnT[:, ks] = v.wdn[ks].T
 
-    pl.semaphore_wait(barrier, len(peers))
-    for r in range(R):
-        announce(0, r)
-
     need("wout", "bout", "ln2g", "ln2b", "bup", "bdn", "cot")
     ln2g, ln2b = v.ln2g[...], v.ln2b[...]
 
-    def forward_attention(a, r, bias, s_scr, nb):
+    def forward_attention(a, r, bias, s_scr, qT_s, nb):
         KB = nb * L
-        length = v.lengths[r]
         rows = v.nall[a, r, 0:KB, :]
         keys = nn(rows, v.wqkv[:, D:2 * D]).astype(BF)
-        qT = v.qT[...]
-        for t in range(nb):
-            key_pos = t * L + lax.broadcasted_iota(jnp.int32, (L, L), 0)
-            query_pos = me * L + lax.broadcasted_iota(jnp.int32, (L, L), 1)
-            bias[t * L:(t + 1) * L] = jnp.where((key_pos <= query_pos) & (key_pos < length), 0.0, MASKED)
+        qT = qT_s[r]
         tops = []
         for h in range(HEADS):
-            s = nn(keys[:, pair(h)], head_rows(qT, h)) + bias[0:KB]
+            s = nn(keys[:, pair(h)], head_rows(qT, h)) + bias[r, 0:KB]
             s_scr[0:KB, h * L:(h + 1) * L] = s
             tops.append(jnp.max(jnp.max(s.reshape(KB // 8, 8, L), axis=0), axis=0, keepdims=True))
         VT = (nt(v.wT[2 * D:], rows) + wide(v.bcol[1], KB)).astype(BF)
@@ -376,18 +406,29 @@
             v.linv[a, r, h] = jnp.broadcast_to(inv, (8, L))
             v.oT[a, r, hs] = (sum(out) * inv).astype(BF)
 
-    def forward_all(bias, s_scr):
+    def forward_all(bias, s_scr, qT_s):
+        def queries(a, r):
+            normed = v.nall[a, r, mine]
+            qT = ((nt(v.wT[:D], normed) + wide(v.bcol[0], L)) * (HD ** -0.5)).astype(BF)
+            v.qn[a, r] = qT.T
+            qT_s[r] = qT
+
+        @pl.loop(0, R)
+        def _(r):
+            queries(0, r)
+            length = v.lengths[r]
+            for t in range(S):
+                key_pos = t * L + lax.broadcasted_iota(jnp.int32, (L, L), 0)
+                query_pos = me * L + lax.broadcasted_iota(jnp.int32, (L, L), 1)
+                bias[r, t * L:(t + 1) * L] = jnp.where((key_pos <= query_pos) & (key_pos < length), 0.0, MASKED)
+
         hand_on(0, 0)
 
         @pl.loop(0, 2 * R)
         def _(n):
             a, r = lax.div(n, R), lax.rem(n, R)
-            normed = v.nall[a, r, mine]
-            qT = ((nt(v.wT[:D], normed) + wide(v.bcol[0], L)) * (HD ** -0.5)).astype(BF)
-            v.qn[a, r] = qT.T
-            v.qT[...] = qT
             gathered(a, r)
-            with_size(functools.partial(forward_attention, a, r, bias, s_scr))
+            with_size(functools.partial(forward_attention, a, r, bias, s_scr, qT_s))
 
             @pl.when(n < 2 * R - 1)
             def _():
@@ -409,6 +450,7 @@
             def _():
                 first_norm(1, r)
                 announce(1, r)
+                queries(1, r)
 
             @pl.when(a == 1)
             def _():
@@ -417,7 +459,9 @@
                 out_copy(v, 0, v.hid, v.y, r).start()
 
     VM = pltpu.VMEM
-    pl.run_scoped(forward_all, VM((S * L, L), F32), VM((S * L, HEADS * L), F32))
+    if reduce_here:
+        v.passed_on = passed_on
+    pl.run_scoped(forward_all, VM((R, S * L, L), F32), VM((S * L, HEADS * L), F32), VM((R, D, L), BF))
     pl.run_scoped(functools.partial(backward, v, with_size), VM((R, D, L), BF), VM((R, L, FF), BF), VM((R, L, D), BF),
                   VM((R, L, 3 * D), BF), VM((D, W), F32), VM((L, D), F32),
                   VM((S * L, D), BF), VM((S * L, 2 * D), BF))
@@ -597,12 +641,13 @@
         up, down, qkv = (Share(v, start, w, into(p), (pair_stage, plane, across), whole)
                          for p, (start, w, whole) in enumerate(((UP, FF, False), (DN, FF + D, False), (QW, 3 * D, True))))
         small = SmallSum(v)
+        v.passed_on()
 
     def nothing():
         pass
 
     def attention(a, r, tick):
-        with_size(functools.partial(attention_core, a, r, tick if reducing else nothing))
+        with_size(functools.partial(attention_core, a, r, tick))
 
     for r in range(R):
         backward_mlp(1, r)
@@ -611,14 +656,10 @@
 
     @pl.loop(0, R)
     def _(r):
-        attention(1, r, nothing)
-
-        @pl.when(r > 0)
-        def _():
-            pass_on(1, r - 1)
-
+        attention(1, r, lambda: pl.when(r > 0)(lambda: pass_on(1, r - 1)))
+
+    pass_on(1, R - 1)
     query_terms(1)
-    pass_on(1, R - 1)
 
     def between(r):
         backward_norm(1, r)
@@ -640,11 +681,13 @@
     sent(1)
 
     def tick_first():
-        up.step(0)
-        down.step(0)
+        if reducing:
+            up.step(0)
+            down.step(0)
 
     def tick_last():
-        up.step(1)
+        if reducing:
+            up.step(1)
 
     for r in range(R):
         attention(0, r, tick_first if r == 0 else tick_last if r == R - 1 else nothing)
@@ -755,14 +798,14 @@
         X, Z = S // 2, DP // 2
         parts = (FF, FF + D, 3 * D)
         members, wholes = (2, S, Z), (False, False, True)
-        reduce_here = DP % 2 == 0 and Z > 1 and all(share_plan(D, w, members, f) for w, f in zip(parts, wholes))
+        reduce_here = DP % 2 == 0 and 1 < Z <= 4 and all(share_plan(D, w, members, f) for w, f in zip(parts, wholes))
         cfg = (S, DP, R, L, D, FF, reduce_here)
         VM = pltpu.VMEM
         DMA = pltpu.SemaphoreType.DMA
         scratch = dict(
             wT=VM((3 * D, D), BF), wupT=VM((FF, D), BF), wdnT=VM((D, FF), BF), bcol=VM((2, D, 128), F32),
             stream=VM((R, L, D), F32), gstream=VM((R, L, D), F32), gmid=VM((R, L, D), F32), nall=VM((2, R, S * L, D), BF), xh1=VM((2, R, L, D), F32), rs1=VM((2, R, L, 128), F32),
-            xh2=VM((2, R, L, D), F32), rs2=VM((2, R, L, 128), F32), n2T=VM((2, R, D, L), BF), qT=VM((D, L), BF),
+            xh2=VM((2, R, L, D), F32), rs2=VM((2, R, L, 128), F32), n2T=VM((2, R, D, L), BF),
             qn=VM((2, R, L, D), BF), linv=VM((2, R, HEADS, 8, L), F32), oT=VM((2, R, D, L), BF),
             hidden=VM((2, R, L, FF), BF), slope=VM((2, R, L, FF), F32), e_scr=VM((2, R, S * L, HEADS * L), BF),
             pair_out=VM((R, X - 1, L, D), BF), pair_in=VM((2, R, X - 1, L, D), BF), part_out=VM((R, X - 1, L, D), BF),
@@ -775,7 +818,7 @@
             scratch.update(
                 stage=VM((D, W), BF), gath=VM((D, W), BF), vs1=VM((2, lines, 128), F32), vs2=VM((S, lines, 128), F32),
                 vs3=VM((Z, lines, 128), F32), vss1=DMA((1,)), vsr1=DMA((1,)), vss2=DMA((S - 1,)), vsr2=DMA((S - 1,)),
-                vss3=DMA((Z - 1,)), vsr3=DMA((Z - 1,)))
+                vss3=DMA((Z - 1,)), vsr3=DMA((Z - 1,)), relay=pltpu.SemaphoreType.REGULAR((5,)))
             most = max(S, Z) - 1
             for p, (w, f) in enumerate(zip(parts, wholes)):
                 for k, dims in enumerate(part_shapes(D, w, members, f)):

time: 92.9 us -> 91.7 us (0.987)
  Pallas kernels: 91.9 us -> 90.7 us
    pallas_call x1, Pallas kernels: 87.6 us -> 86.4 us  [shards(): pl.pallas_call(functools.partial(block_kernel, cfg, names), out_shape=tup...]
where the time goes in v4:
time: 91.7 us; the launch traced here: 91.5 us
  Pallas kernels  90.7 us (99%)
    pallas_call x1, Pallas kernels, shards(): pl.pallas_call(functools.partial(block_kernel, cfg, names), out_shape=tup...  86.4 us
    pallas_call x1, Pallas kernels, shards(): pl.pallas_call(functools.partial(finish_kernel, D, FF, (*outs, *ends, *te...  4.3 us

profile of v4, /device:TPU:0, one launch (start us, length us, event | category | flops | bytes accessed | tf_op | source)
XLA Modules:
  0.0 91.5 jit_solution(12947885676263729732)
XLA Ops:
  0.7 86.4 %shard_map.271 = (bf16[3,256,256]{2,1,0:T(8,128)(2,1)}, f32[3,256,256]{2,1,0:T(8,128)}, f32[3,256,256]{2,1,0:T(8,128)}, bf16[256,3072]{1,0:T(8,128)(2,1)}, f32[24,128]{1,0:T(8,128)}) custom-call(bf16[3,256,256]{2,1,0:T(8,128)(2,1)} %bitcast.20, bf16[3,256,256]{2,1,0:T(8,128)(2,1)} %bitcast.21, bf16[3,256,256]{2,1,0:T(8,128)(2,1)} %bitcast.22, s32[3]{0:T(128)} %refs_3_.1, ...), custom_call_target="tpu_custom_call" | custom-call | tf_op jit(solution)/shard_map/pallas_call | solution.py:842
  87.0 4.3 %shard_map.272 = (bf16[3,256,256]{2,1,0:T(8,128)(2,1)}, f32[3,256,256]{2,1,0:T(8,128)}, f32[3,256,256]{2,1,0:T(8,128)}, f32[1,256]{1,0:T(1,128)}, f32[1,256]{1,0...) custom-call(bf16[3,256,256]{2,1,0:T(8,128)(2,1)} %get-tuple-element., ...), custom_call_target="tpu_custom_call" | custom-call | tf_op jit(solution)/shard_map/pallas_call | solution.py:859

commit v5 on v4

--- a/solution.py
+++ b/solution.py
@@ -719,9 +719,9 @@
         up.step(2)
         qkv.step(1)
         down.step(2)
+        up.step(3)
         final(R - 1)
         small.start(0, small_lines())
-        up.step(3)
         small.start(1, small.finish(0))
         qkv.step(2)
         down.step(3)

time: 91.7 us -> 91.7 us (level)
  no operation moved by 1% of the time
where the time goes in v5:
time: 91.7 us; the launch traced here: 91.5 us
  Pallas kernels  90.7 us (99%)
    pallas_call x1, Pallas kernels, shards(): pl.pallas_call(functools.partial(block_kernel, cfg, names), out_shape=tup...  86.4 us
    pallas_call x1, Pallas kernels, shards(): pl.pallas_call(functools.partial(finish_kernel, D, FF, (*outs, *ends, *te...  4.3 us

profile of v5, /device:TPU:0, one launch (start us, length us, event | category | flops | bytes accessed | tf_op | source)
XLA Modules:
  0.0 91.5 jit_solution(7785729493222281755)
XLA Ops:
  0.7 86.4 %shard_map.271 = (bf16[3,256,256]{2,1,0:T(8,128)(2,1)}, f32[3,256,256]{2,1,0:T(8,128)}, f32[3,256,256]{2,1,0:T(8,128)}, bf16[256,3072]{1,0:T(8,128)(2,1)}, f32[24,128]{1,0:T(8,128)}) custom-call(bf16[3,256,256]{2,1,0:T(8,128)(2,1)} %bitcast.20, bf16[3,256,256]{2,1,0:T(8,128)(2,1)} %bitcast.21, bf16[3,256,256]{2,1,0:T(8,128)(2,1)} %bitcast.22, s32[3]{0:T(128)} %refs_3_.1, ...), custom_call_target="tpu_custom_call" | custom-call | tf_op jit(solution)/shard_map/pallas_call | solution.py:842
  87.0 4.3 %shard_map.272 = (bf16[3,256,256]{2,1,0:T(8,128)(2,1)}, f32[3,256,256]{2,1,0:T(8,128)}, f32[3,256,256]{2,1,0:T(8,128)}, f32[1,256]{1,0:T(1,128)}, f32[1,256]{1,0...) custom-call(bf16[3,256,256]{2,1,0:T(8,128)(2,1)} %get-tuple-element., ...), custom_call_target="tpu_custom_call" | custom-call | tf_op jit(solution)/shard_map/pallas_call | solution.py:859
